TPU v7x, 32 devices: a whole 2x2x4 slice. The times are simulated.
32 devices in a mesh: row: 4 (over y, x), seq: 8 (over z, core).
Axes of the slice: x: 2, y: 2, z: 4, core: 2. Of those that a mesh axis runs over, the one named last changes fastest.
Arguments:
- hidden_in: bfloat16 [8, 2048, 1024], P('row', 'seq'), may hold values from -6 to 6
- lengths: int32 [8, 8], P('row'), may hold values from 1 to 2041, as said below
- norm1_gain: bfloat16 [1024], replicated, may hold values from 0.5 to 1.5
- w_qkv: bfloat16 [1024, 5120], replicated, may hold values from -0.1875 to 0.1875
- conv_w: bfloat16 [5120, 4], replicated, may hold values from -3 to 3
- w_rates: bfloat16 [1024, 24], replicated, may hold values from -0.1875 to 0.1875
- a_log: float32 [8], replicated, may hold values from -6.5 to -2.5
- dt_bias: float32 [8], replicated, may hold values from -1 to 1
- w_gate: bfloat16 [1024, 1024], replicated, may hold values from -0.1875 to 0.1875
- out_gain: bfloat16 [128], replicated, may hold values from 0.5 to 1.5
- w_out: bfloat16 [1024, 1024], replicated, may hold values from -0.25 to 0.25
- norm2_gain: bfloat16 [1024], replicated, may hold values from 0.5 to 1.5
- w_up: bfloat16 [1024, 5632], replicated, may hold values from -0.1875 to 0.1875
- w_down: bfloat16 [2816, 1024], replicated, may hold values from -0.15625 to 0.15625
- cotangent: bfloat16 [8, 2048, 1024], P('row', 'seq'), may hold values from -6 to 6
Outputs:
- layer_out: bfloat16 [8, 2048, 1024], P('row', 'seq')
- grad_x: bfloat16 [8, 2048, 1024], P('row', 'seq')
- grad_norm1_gain: float32 [1024], P('seq')
- grad_w_qkv: float32 [1024, 5120], P('seq')
- grad_conv_w: float32 [5120, 4], P('seq')
- grad_w_rates: float32 [1024, 24], P('seq')
- grad_a_log: float32 [8], replicated
- grad_dt_bias: float32 [8], replicated
- grad_w_gate: float32 [1024, 1024], P('seq')
- grad_out_gain: float32 [128], replicated
- grad_w_out: float32 [1024, 1024], P('seq')
- grad_norm2_gain: float32 [1024], P('seq')
- grad_w_up: float32 [1024, 5632], P('seq')
- grad_w_down: float32 [2816, 1024], P('seq')
Inputs may be any that keep to these rules, and one draw needn't show every extreme that they name: Each row's 8 lengths are positive and sum to 2048; documents are laid end to end in the order given.
All inputs are finite; a program needn't handle non-finite values.
Results may differ from a plain program's by a relative error of at most 0.02.
Values may be sent and summed in bfloat16 or wider, within the bound.
No kernel may reach another device: no remote copies, remote signals or barrier semaphores. Data moves between devices by JAX's collectives and lax.ppermute only.
A program may use at most 384 MiB of HBM per device.

v0:
```python
from functools import partial

import jax
import jax.numpy as jnp
from jax import lax
from jax.sharding import PartitionSpec as P

D = 1024
HEADS = 8
HDIM = 128
NH = 2
FF = 2816
BLOCK = 64


EPSILON = 1e-06
HIGHEST = lax.Precision.HIGHEST


def passed_along(value, axis, steps):
    count = lax.axis_size(axis)
    first, last = (max(0, -steps), min(count, count - steps))
    return lax.ppermute(value, axis, [(source, source + steps) for source in range(first, last)])


def prefix(value, axis, combine, identity):
    peers, position = (lax.axis_size(axis), lax.axis_index(axis))
    everything = jax.tree.map(
        lambda part, kind: lax.all_gather(part.astype(kind), axis),
        value,
        (jnp.bfloat16, jnp.bfloat16),
    )
    start = jax.tree.map(
        lambda part, zero: jnp.broadcast_to(jnp.asarray(zero, part.dtype), part.shape),
        value,
        identity,
    )

    def hop(k, before):
        reached = k < position
        new = combine(
            before, jax.tree.map(lambda part, own: part[k].astype(own.dtype), everything, value)
        )
        return jax.tree.map(lambda a, b: jnp.where(reached, a, b), new, before)

    return lax.fori_loop(0, peers, hop, start)


def prefix_2(value, axis, combine, identity):
    peers, position = (lax.axis_size(axis), lax.axis_index(axis))
    everything = jax.tree.map(
        lambda part, kind: lax.all_gather(part.astype(kind), axis),
        value,
        jax.tree.map(lambda a: jnp.bfloat16 if a.dtype == jnp.float32 else a.dtype, value),
    )
    start = jax.tree.map(
        lambda part, zero: jnp.broadcast_to(jnp.asarray(zero, part.dtype), part.shape),
        value,
        identity,
    )

    def hop(k, before):
        at = peers - 1 - k
        reached = at > position
        new = combine(
            before, jax.tree.map(lambda part, own: part[at].astype(own.dtype), everything, value)
        )
        return jax.tree.map(lambda a, b: jnp.where(reached, a, b), new, before)

    return lax.fori_loop(0, peers, hop, start)


def shortened(value):

    def short(part):
        return part.astype(jnp.bfloat16) if part.dtype == jnp.float32 else part

    return jax.tree.map(short, value)


def full_product(formula, former, latter):
    return jnp.einsum(formula, former, latter, precision=HIGHEST)


def half_product(formula, former, latter):
    return jnp.einsum(formula, former, latter, preferred_element_type=jnp.float32)


def rounded(tensor):
    return lax.optimization_barrier(tensor.astype(jnp.bfloat16)).astype(jnp.float32)


def rms_norm(tensor, gain):
    return tensor * lax.rsqrt(jnp.mean(tensor * tensor, axis=-1, keepdims=True) + EPSILON) * gain


def unit_rows(tensor):
    return tensor * lax.rsqrt(jnp.sum(tensor * tensor, axis=-1, keepdims=True) + EPSILON)


def find_docs(doc_ends, places):
    found = jnp.sum((places[None, :, None] >= doc_ends[:, None, :]).astype(jnp.int32), axis=2)
    return jnp.where(places[None, :] >= 0, found, -1)


def front_terms(extended, conv_float, keep_taps):
    row_count = keep_taps.shape[0]
    length = keep_taps.shape[1]
    summed = extended[:, 0:length] * keep_taps[..., 0:1] * conv_float[:, 0]
    for offset in range(1, keep_taps.shape[2]):
        summed = (
            summed
            + extended[:, offset : offset + length]
            * keep_taps[..., offset : offset + 1]
            * conv_float[:, offset]
        )
    active = jax.nn.silu(summed)
    query = unit_rows(active[..., :D].reshape(row_count, length, HEADS, HDIM))
    key_rows = unit_rows(active[..., D : D + NH * D].reshape(row_count, length * NH, HEADS, HDIM))
    values = active[..., D + NH * D :].reshape(row_count, length * NH, HEADS, HDIM)
    return (query, key_rows, values)


def rate_terms(rate_logits, a_log, dt_bias):
    row_count = rate_logits.shape[0]
    length = rate_logits.shape[1]
    beta_rows = jax.nn.sigmoid(rate_logits[..., : NH * HEADS]).reshape(
        row_count, length * NH, HEADS
    )
    log_rate = -jnp.exp(a_log) * jax.nn.softplus(rate_logits[..., NH * HEADS :] + dt_bias)
    padding = jnp.zeros((row_count, length, NH - 1, HEADS), jnp.float32)
    log_decay = jnp.concatenate([log_rate[:, :, None, :], padding], axis=2).reshape(
        row_count, length * NH, HEADS
    )
    return (beta_rows, log_decay)


def to_blocks(tensor, block_count):
    sizes_of = tensor.shape
    reshaped = tensor.reshape((sizes_of[0], block_count, sizes_of[1] // block_count) + sizes_of[2:])
    return jnp.moveaxis(reshaped, 2, 3)


def chain_maps(earlier, later):
    return (
        full_product("rhab,rhbc->rhac", earlier[0], later[0]),
        full_product("rhva,rhab->rhvb", earlier[1], later[0]) + later[1],
    )


def block_maps(key_rows, values, beta_rows, log_decay, doc_virtual, doc_before):
    row_count = key_rows.shape[0]
    block_count = doc_before.shape[1]
    span_len = key_rows.shape[1] // block_count
    key_blocks = to_blocks(key_rows, block_count)
    key_low = key_blocks.astype(jnp.bfloat16)
    value_blocks = to_blocks(values, block_count)
    beta_blocks = to_blocks(beta_rows, block_count)
    summed_log = jnp.cumsum(to_blocks(log_decay, block_count), axis=-1)
    doc_blocks = doc_virtual.reshape(row_count, block_count, span_len)
    indices = jnp.arange(span_len)
    same_doc = (doc_blocks[..., :, None] == doc_blocks[..., None, :])[:, :, None]
    lower_mask = indices[:, None] >= indices[None, :]
    strict_mask = (indices[:, None] > indices[None, :]).astype(jnp.float32)
    decay = jnp.exp(
        jnp.where(
            same_doc & lower_mask, summed_log[..., :, None] - summed_log[..., None, :], -jnp.inf
        )
    )
    carry_on = (doc_blocks == doc_before[..., None]).astype(jnp.float32)[:, :, None]
    start_decay = jnp.exp(summed_log) * carry_on
    weighted = beta_blocks[..., None] * key_blocks
    mixing = (
        beta_blocks[..., :, None]
        * half_product("...tk,...sk->...ts", key_low, key_low)
        * decay
        * strict_mask
    )
    right_side = jnp.concatenate(
        [start_decay[..., None] * weighted, beta_blocks[..., None] * value_blocks], axis=-1
    )
    solved = jax.scipy.linalg.solve_triangular(mixing, right_side, lower=True, unit_diagonal=True)
    wide_keys = solved[..., :HDIM]
    fresh_values = solved[..., HDIM:]
    tail_keys = decay[..., -1, :, None] * key_blocks
    identity = jnp.eye(HDIM, dtype=jnp.float32)
    block_m = start_decay[..., -1, None, None] * identity - full_product(
        "...sa,...sb->...ab", wide_keys, tail_keys
    )
    block_b = full_product("...sv,...sk->...vk", fresh_values, tail_keys)

    def compose(carried, block_pair):
        return (chain_maps(carried, block_pair), carried)

    initial = (
        jnp.broadcast_to(identity, block_m[:, 0].shape),
        jnp.zeros(block_b[:, 0].shape, jnp.float32),
    )
    (device_m, device_b), (prefix_m, prefix_b) = lax.scan(
        compose, initial, (jnp.moveaxis(block_m, 1, 0), jnp.moveaxis(block_b, 1, 0))
    )
    return (
        decay,
        start_decay,
        wide_keys,
        fresh_values,
        jnp.moveaxis(prefix_m, 0, 1),
        jnp.moveaxis(prefix_b, 0, 1),
        device_m,
        device_b,
    )


def finish(query, key_rows, block_data, state_in):
    decay, start_decay, wide_keys, fresh_values, prefix_m, prefix_b, device_m, device_b = block_data
    row_count = query.shape[0]
    length = query.shape[1]
    block_count = prefix_m.shape[1]
    query_blocks = to_blocks(query, block_count)
    key_blocks = to_blocks(key_rows, block_count)
    block_starts = full_product("rhvk,rnhka->rnhva", state_in, prefix_m) + prefix_b
    delta_rows = fresh_values - full_product("...sk,...vk->...sv", wide_keys, block_starts)
    scores = (
        half_product(
            "...tk,...sk->...ts", query_blocks.astype(jnp.bfloat16), key_blocks.astype(jnp.bfloat16)
        )
        * decay[..., NH - 1 :: NH, :]
    )
    output = start_decay[..., NH - 1 :: NH, None] * full_product(
        "...tk,...vk->...tv", query_blocks, block_starts
    )
    output = output + full_product("...ts,...sv->...tv", scores, delta_rows)
    output = jnp.moveaxis(output, 3, 2).reshape(row_count, length, HEADS, HDIM)
    return output


def gated_norm(mixed, out_gain, gate_logits):
    return rms_norm(mixed, out_gain) * jax.nn.silu(gate_logits.reshape(mixed.shape))


def swiglu(gate_up):
    return jax.nn.silu(gate_up[..., :FF]) * gate_up[..., FF:]


def local(
    hidden_in,
    lengths,
    norm1_gain,
    w_qkv,
    conv_w,
    w_rates,
    a_log,
    dt_bias,
    w_gate,
    out_gain,
    w_out,
    norm2_gain,
    w_up,
    w_down,
    cotangent,
):
    row_count = hidden_in.shape[0]
    length = hidden_in.shape[1]
    halo_rows = conv_w.shape[1] - 1
    anchor = lax.axis_index("seq") * length
    doc_ends = jnp.cumsum(lengths, axis=1)
    doc_extended = find_docs(doc_ends, anchor + jnp.arange(-halo_rows, length, dtype=jnp.int32))
    doc_tokens = doc_extended[:, halo_rows:]
    keep_taps = jnp.stack(
        [
            (doc_extended[:, offset : offset + length] == doc_tokens).astype(jnp.float32)
            for offset in range(halo_rows + 1)
        ],
        axis=-1,
    )
    doc_virtual = jnp.repeat(doc_tokens, NH, axis=1)
    doc_before = find_docs(doc_ends, anchor + jnp.arange(0, length, BLOCK, dtype=jnp.int32) - 1)
    input_float = hidden_in.astype(jnp.float32)
    normed_float, norm1_back = jax.vjp(rms_norm, input_float, norm1_gain.astype(jnp.float32))
    normed = normed_float.astype(jnp.bfloat16)
    projected = half_product("rld,de->rle", normed, w_qkv).astype(jnp.bfloat16)
    rate_logits = half_product("rld,de->rle", normed, w_rates)
    gate_logits = half_product("rld,de->rle", normed, w_gate)
    incoming = passed_along(projected[:, length - halo_rows :], "seq", 1)
    extended = jnp.concatenate([incoming, projected], axis=1).astype(jnp.float32)
    front, front_back = jax.vjp(
        partial(front_terms, keep_taps=keep_taps), extended, conv_w.astype(jnp.float32)
    )
    query, key_rows, values = [rounded(member) for member in front]
    (beta_rows, log_decay), rate_back = jax.vjp(rate_terms, rate_logits, a_log, dt_bias)
    block_data, maps_back = jax.vjp(
        partial(block_maps, doc_virtual=doc_virtual, doc_before=doc_before),
        key_rows,
        values,
        beta_rows,
        log_decay,
    )
    identity = jnp.broadcast_to(jnp.eye(HDIM, dtype=jnp.float32), block_data[6].shape)
    nothing = jnp.zeros(block_data[7].shape, jnp.float32)
    state_in = prefix((block_data[6], block_data[7]), "seq", chain_maps, (identity, nothing))[1]
    mixed, finish_back = jax.vjp(finish, query, key_rows, block_data, state_in)
    branch_float, branch_back = jax.vjp(
        gated_norm, mixed, out_gain.astype(jnp.float32), gate_logits
    )
    branch = branch_float.reshape(row_count, length, D).astype(jnp.bfloat16)
    hidden = input_float + half_product("rld,de->rle", branch, w_out)
    normed2_float, norm2_back = jax.vjp(rms_norm, hidden, norm2_gain.astype(jnp.float32))
    normed2 = normed2_float.astype(jnp.bfloat16)
    gate_up = half_product("rld,de->rle", normed2, w_up)
    activated_float, swiglu_back = jax.vjp(swiglu, gate_up)
    activated = activated_float.astype(jnp.bfloat16)
    layer_out = (hidden + half_product("rlf,fd->rld", activated, w_down)).astype(jnp.bfloat16)
    grad_w_down = half_product("rlf,rld->fd", activated, cotangent)
    grad_act = half_product("rld,fd->rlf", cotangent, w_down)
    grad_gate_up = swiglu_back(grad_act)[0].astype(jnp.bfloat16)
    grad_w_up = half_product("rld,rle->de", normed2, grad_gate_up)
    grad_normed2 = half_product("rle,de->rld", grad_gate_up, w_up)
    grad_hidden_part, grad_norm2_gain = norm2_back(grad_normed2)
    grad_hidden = cotangent.astype(jnp.float32) + grad_hidden_part
    mlp_terms = (grad_norm2_gain, grad_w_up, grad_w_down)
    grad_attended = grad_hidden.astype(jnp.bfloat16)
    grad_w_out = half_product("rld,rle->de", branch, grad_attended)
    grad_branch = half_product("rle,de->rld", grad_attended, w_out).reshape(
        row_count, length, HEADS, HDIM
    )
    grad_mixed, grad_out_gain, grad_gate_float = branch_back(grad_branch)
    grad_gate = grad_gate_float.astype(jnp.bfloat16)
    grad_query_first, grad_keys_first, grad_maps_first, grad_state_local = finish_back(grad_mixed)
    transposed = jnp.swapaxes(block_data[6], -1, -2)
    adjoint = prefix_2((transposed, grad_state_local), "seq", chain_maps, (identity, nothing))[1]
    grad_device_m = full_product("rhvk,rhva->rhka", state_in, adjoint)
    grad_maps = grad_maps_first[:6] + (
        grad_maps_first[6] + grad_device_m,
        grad_maps_first[7] + adjoint,
    )
    grad_keys_maps, grad_values_float, grad_beta, grad_log_decay = maps_back(grad_maps)
    grad_query = rounded(grad_query_first)
    grad_keys = rounded(grad_keys_first + grad_keys_maps)
    grad_values = rounded(grad_values_float)
    grad_rates_float, grad_a_log, grad_dt_bias = rate_back((grad_beta, grad_log_decay))
    grad_rates = grad_rates_float.astype(jnp.bfloat16)
    grad_extended, grad_conv_w = front_back((grad_query, grad_keys, grad_values))
    returned = passed_along(grad_extended[:, :halo_rows].astype(jnp.bfloat16), "seq", -1).astype(
        jnp.float32
    )
    grad_projected = grad_extended[:, halo_rows:] + jnp.pad(
        returned, ((0, 0), (length - halo_rows, 0), (0, 0))
    )
    grad_projected = grad_projected.astype(jnp.bfloat16)
    grad_w_qkv = half_product("rld,rle->de", normed, grad_projected)
    grad_w_rates = half_product("rld,rle->de", normed, grad_rates)
    grad_w_gate = half_product("rld,rle->de", normed, grad_gate)
    grad_normed = half_product("rle,de->rld", grad_projected, w_qkv)
    grad_normed = grad_normed + half_product("rle,de->rld", grad_rates, w_rates)
    grad_normed = grad_normed + half_product("rle,de->rld", grad_gate, w_gate)
    grad_input_part, grad_norm1_gain = norm1_back(grad_normed)
    grad_x = (grad_hidden + grad_input_part).astype(jnp.bfloat16)
    small_terms = (grad_a_log, grad_dt_bias, grad_out_gain)
    mixer_terms = (grad_norm1_gain, grad_w_qkv, grad_conv_w, grad_w_rates, grad_w_gate, grad_w_out)
    small_sums = lax.psum((small_terms[0], small_terms[1], small_terms[2]), ("row", "seq"))
    shards = jax.tree.map(
        lambda part: part.astype(jnp.float32),
        lax.psum_scatter(
            shortened(mlp_terms + mixer_terms), "seq", scatter_dimension=0, tiled=True
        ),
    )
    totals = jax.tree.map(lambda part: part.astype(jnp.float32), lax.psum(shortened(shards), "row"))
    return (
        layer_out,
        grad_x,
        totals[3],
        totals[4],
        totals[5],
        totals[6],
        small_sums[0],
        small_sums[1],
        totals[7],
        small_sums[2],
        totals[8],
        totals[0],
        totals[1],
        totals[2],
    )


def solution(mesh):
    return jax.shard_map(
        local,
        mesh=mesh,
        in_specs=(
            P("row", "seq", None),
            P("row", None),
            P(),
            P(),
            P(),
            P(),
            P(),
            P(),
            P(),
            P(),
            P(),
            P(),
            P(),
            P(),
            P("row", "seq", None),
        ),
        out_specs=(
            P("row", "seq", None),
            P("row", "seq", None),
            P("seq"),
            P("seq", None),
            P("seq", None),
            P("seq", None),
            P(),
            P(),
            P("seq", None),
            P(),
            P("seq", None),
            P("seq"),
            P("seq", None),
            P("seq", None),
        ),
        check_vma=False,
    )
```

profile of v0, /device:TPU:0, one launch (start us, length us, event | category | flops | bytes accessed | tf_op | source)
XLA Modules:
  0.0 1820.0 jit_solution(15220125882491489531)
XLA Ops:
  10.2 10.1 fusion.62
  43.9 9.4 fusion.57
  60.2 4.9 reshape.387
  85.7 7.8 add_bitcast_fusion
  93.5 630.3 %custom-call.10 = f32[2,4,8,1,128,128]{4,5,3,2,1,0:T(8,128)} custom-call(f32[2,4,8,1,128,128]{5,4,3,2,1,0:T(8,128)} %get-tuple-element.802), custom_call_target="InvertDiagBlocksLowerTriangular" | custom-call | tf_op jit(solution)/shard_map/jvp(jit(_solve_triangular))/vmap(vmap(vmap()))/triangular_solve | solution.py:182
  724.8 11.8 fusion.58
  736.7 9.6 fusion.131
  746.3 11.1 bitcast_subtract_fusion
  762.6 62.2 %while.68 = (s32[]{:T(128)}, f32[2,8,128,128]{2,3,1,0:T(8,128)S(1)}, f32[2,8,128,128]{2,3,1,0:T(8,128)}, f32[4,2,8,128,128]{3,4,2,1,0:T(8,128)}, f32[4,2,8,128,1...) while((s32[]{:T(128)}, ...), condition=%wide.region_8.9_spmd.clone, body=%wide.region_7.8_spmd.clone.sunk | while | flops 806092800 | bytes 28313248 | solution.py:199
  832.4 9.8 slice.128
  851.2 6.1 fusion.294
  857.4 17.8 all-gather.9.cloned.1.call-done
  875.2 48.1 %all-gather.11.cloned.1.call-done = bf16[16,8,128,128]{3,2,1,0:T(8,128)(2,1)} async-done(((bf16[2,8,128,128]{3,2,1,0:T(8,128)(2,1)}), bf16[16,8,128,128]{3,2,1,0:T(8,128)(2,1)}) %all-gather.11.cloned.1.call-update) | async-done | bytes 4194320 | tf_op jit(solution)/shard_map/all_gather | solution.py:29
  923.2 49.5 %while.69 = (s32[]{:T(128)}, f32[2,8,128,128]{2,3,1,0:T(8,128)S(1)}, s32[]{:T(128)}, bf16[8,2,8,128,128]{4,3,2,1,0:T(8,128)(2,1)}, bf16[8,2,8,128,128]{4,3,2,1,0:T(8,128)(2,1)}, /*index=5*/s32[]{:T(128)}, s32[]{:T(128)}) while((s32[]{:T(128)}, f32[2,8,128,128]{2,3,1,0:T(8,128)S(1)}, s32[]{:T(128)}, ...), condition=%wide.region_10.11_spmd.clone, body=%wide.region_9.10_spmd.clone.sunk | while | flops 403963904 | bytes 8390755 | solution.py:46
  972.7 6.5 bitcast_add_fusion
  981.4 7.6 slice_subtract_fusion
  989.0 5.2 multiply_reduce_fusion.12
  1005.9 5.7 multiply_convert_fusion.4
  1014.3 13.4 fusion.48
  1027.7 11.4 fusion.237
  1039.1 14.4 multiply_reduce_fusion.6
  1067.9 7.0 fusion.296
  1075.0 7.7 fusion.110
  1088.9 5.0 fusion.219
  1102.0 6.9 bitcast_convert_fusion.2
  1109.1 13.3 fusion.295
  1126.0 8.2 fusion.209
  1138.6 4.8 add_add_fusion.2
  1146.2 9.9 fusion.140
  1156.1 10.4 fusion.108
  1166.5 13.5 bitcast_convert_fusion
  1180.5 32.5 %pad.90 = f32[2,4,8,128,128]{4,3,2,1,0:T(8,128)} pad(f32[2,4,8,64,128]{4,3,2,1,0:T(8,128)} %get-tuple-element.825, f32[]{:T(128)} %constant.194.clone.1), padding=0_0_0x0_0_0x0_0_0x1_0_1x0_0_0 | pad | bytes 6291460 | tf_op jit(solution)/shard_map/transpose(jvp())/pad | solution.py:227
  1213.0 34.7 %while.70 = (s32[]{:T(128)}, f32[2,8,128,128]{2,3,1,0:T(8,128)S(1)}, s32[]{:T(128)}, bf16[8,2,8,128,128]{4,3,2,1,0:T(8,128)(2,1)}, bf16[8,2,8,128,128]{4,3,2,1,0...) while((s32[]{:T(128)}, f32[2,8,128,128]{2,3,1,0:T(8,128)S(1)}, s32[]{:T(128)}, ...), condition=%wide.region_16.17_spmd.clone, body=%wide.region_15.16_spmd.clone.sunk | while | flops 403963904 | bytes 8390817 | solution.py:70
  1256.0 73.6 %while.67 = (s32[]{:T(128)}, f32[2,8,128,128]{2,3,1,0:T(8,128)}, f32[2,8,128,128]{2,3,1,0:T(8,128)S(1)}, f32[4,2,8,128,128]{4,3,2,1,0:T(8,128)}, f32[4,2,8,128,1...) while((s32[]{:T(128)}, f32[2,8,128,128]{2,3,1,0:T(8,128)}, ...), condition=%wide.region_18.19_spmd, body=%wide.region_17.18_spmd.sunk | while | flops 1611399168 | bytes 30410924 | solution.py:199
  1259.7 4.5 fusion.361
  1278.1 4.5 fusion.361
  1296.6 4.5 fusion.361
  1315.0 4.5 fusion.361
  1329.6 11.5 fusion.91
  1341.2 6.1 fusion.134
  1347.3 10.2 fusion.137
  1357.6 6.1 fusion.143
  1363.7 16.7 fusion.65
  1380.4 11.3 fusion.66
  1391.7 9.8 fusion.80
  1401.6 15.2 multiply_select_fusion
  1416.8 5.8 fusion.106
  1426.6 4.9 fusion.163
  1435.3 7.1 add_add_fusion
  1442.4 4.9 reshape.394
  1447.4 4.4 copy.453
  1456.0 24.0 %multiply_reduce_fusion.3 = (f32[5120]{0:T(1024)S(1)}, f32[5120]{0:T(1024)S(1)}, f32[5120]{0:T(1024)S(1)}, f32[5120]{0:T(1024)}, f32[2,256,5120]{2,1,0:T(8,128)S(1)}) fusion(f32[2,259,5120]{2,1,0:T(8,128)} %copy-done.2, f32[2,256]{1,0:T(2,128)S(1)} %copy-done.109, f32[2,256]{1,0:T(2,128)S(1)} %copy-done.113, f32[2,256]{1,0:T(2,128)S(1)} %copy-done.111, ...), kind=kLoop, calls=%fused_computation.84 | loop fusion | flops 60272640 | bytes 71391232 | tf_op jit(solution)/shard_map/transpose(jvp())/reduce_sum | solution.py:113
  1480.0 15.5 broadcast_multiply_fusion
  1495.5 14.6 pad_add_fusion
  1514.1 8.8 bitcast_convert_fusion.1
  1531.0 9.9 reduce_window_sum.35
  1546.6 87.0 %reduce-scatter.12.cloned.1.call-done = bf16[128,5120]{1,0:T(8,128)(2,1)} async-done(((bf16[1024,5120]{1,0:T(8,128)(2,1)}), bf16[128,5120]{1,0:T(8,128)(2,1)}) %reduce-scatter.12.cloned.1.call-update) | async-done | bytes 1310736 | tf_op jit(solution)/shard_map/reduce_scatter | solution.py:363
  1633.7 4.7 fusion.170
  1638.4 6.9 add_convert_fusion.3
  1645.3 38.3 %all-reduce.25 = (f32[8]{0:T(128)}, f32[8]{0:T(128)}, f32[128]{0:T(128)}) all-reduce(f32[8]{0:T(128)S(1)} %negate_multiply_fusion, f32[8]{0:T(128)S(1)} %get-tuple-element.783, f32[128]{0:T(128)S(1)} %copy-done.130), channel_id=1, replica_groups=mesh['row'=4,'seq'=8] {'row','seq'}, use_global_device_ids=true, to_apply=%region_46.47 | all-reduce | flops 144 | bytes 1152 | tf_op jit(solution)/shard_map/psum | solution.py:360
  1685.4 14.0 fusion.151
  1699.4 14.9 all-reduce.26
  1719.4 15.6 all-reduce.27
  1737.3 67.5 %all-reduce.31.cloned.1.call-done = (bf16[128,5120]{1,0:T(8,128)(2,1)}, bf16[128,1024]{1,0:T(8,128)(2,1)}, bf16[128,1024]{1,0:T(8,128)(2,1)}, bf16[128,5632]{1,0:T(8,128)(2,1)}, bf16[352,1024]{1,0:T(8,128)(2,1)}) async-done(((bf16[128,5120]{1,0:T(8,128)(2,1)}, bf16[128,1024]{1,0:T(8,128)(2,1)}, bf16[128,1024]{1,0:T(8,128)(2,1)}, bf16[128,5632]{1,0:T(8,128)(2,1)}, bf16[352,1024]{1,0:T(8,128)(2,1)}), ...) | async-done | bytes 3997712 | tf_op jit(solution)/shard_map/psum | solution.py:367
  (614 shorter events, 388.0 us)
Async XLA Ops:
  7.2 1004.4 %copy-start = (bf16[1024,1024]{1,0:T(8,128)(2,1)S(1)}, bf16[1024,1024]{1,0:T(8,128)(2,1)}, u32[]{:S(2)}) copy-start(bf16[1024,1024]{1,0:T(8,128)(2,1)} %param.33) | copy-start | bytes 6291460
  7.2 868.0 %all-gather.9.cloned.1.call-start = ((), (), s32[]{:S(2)}) async-start(), calls=%async_computation.12 | async-start | bytes 4718592 | tf_op jit(solution)/shard_map/all_gather | solution.py:29
  9.5 23.4 %copy-start.119 = (f32[2,256]{1,0:T(2,128)}, f32[2,256]{1,0:T(2,128)S(1)}, u32[]{:S(2)}) copy-start(f32[2,256]{1,0:T(2,128)S(1)} %fusion.258) | copy-start | bytes 6148
  10.2 22.8 %copy-start.116 = (f32[1024]{0:T(1024)}, f32[1024]{0:T(1024)S(1)}, u32[]{:S(2)}) copy-start(f32[1024]{0:T(1024)S(1)} %convert_element_type.302) | copy-start | bytes 12292
  10.2 16.3 copy-start.127
  10.2 20.2 %copy-start.102 = (bf16[5120,4]{0,1:T(4,128)(2,1)S(1)}, bf16[5120,4]{0,1:T(4,128)(2,1)}, u32[]{:S(2)}) copy-start(bf16[5120,4]{0,1:T(4,128)(2,1)} %param.27) | copy-start | bytes 122884
  10.2 22.8 %copy-start.61 = (bf16[2,256,1024]{2,1,0:T(8,128)(2,1)S(1)}, bf16[2,256,1024]{2,1,0:T(8,128)(2,1)}, u32[]{:S(2)}) copy-start(bf16[2,256,1024]{2,1,0:T(8,128)(2,1)} %param.23) | copy-start | bytes 3145732
  23.3 16.3 collective-permute-start
  27.5 16.3 copy-start.108
  27.5 16.3 copy-start.110
  30.3 716.0 %copy-start.78 = (f32[128,128]{1,0:T(8,128)}, f32[128,128]{1,0:T(8,128)S(1)}, u32[]{:S(2)}) copy-start(f32[128,128]{1,0:T(8,128)S(1)} %fusion.242) | copy-start | bytes 196612
  31.0 12.8 copy-start.94
  31.0 12.8 copy-start.96
  36.6 46.6 %copy-start.82 = (f32[2,4,8,128]{3,2,1,0:T(8,128)}, f32[2,4,8,128]{3,2,1,0:T(8,128)S(1)}, u32[]{:S(2)}) copy-start(f32[2,4,8,128]{3,2,1,0:T(8,128)S(1)} %copy.407) | copy-start | bytes 98308
  36.9 46.2 %copy-start.72 = (pred[2,4,128,128]{3,2,1,0:T(8,128)(4,1)}, pred[2,4,128,128]{3,2,1,0:T(8,128)(4,1)S(1)}, u32[]{:S(2)}) copy-start(pred[2,4,128,128]{3,2,1,0:T(8,128)(4,1)S(1)} %compare_and_fusion) | copy-start | bytes 393220
  37.0 46.2 %copy-start.76 = (f32[128,128]{1,0:T(8,128)}, f32[128,128]{1,0:T(8,128)S(1)}, u32[]{:S(2)}) copy-start(f32[128,128]{1,0:T(8,128)S(1)} %get-tuple-element.830) | copy-start | bytes 196612
  37.1 46.2 %copy-start.87 = (pred[128,128]{1,0:T(8,128)(4,1)}, pred[128,128]{1,0:T(8,128)(4,1)S(1)}, u32[]{:S(2)}) copy-start(pred[128,128]{1,0:T(8,128)(4,1)S(1)} %get-tuple-element.829) | copy-start | bytes 49156
  39.4 43.8 %copy-start.67 = (f32[2,4,8,128]{3,2,1,0:T(8,128)}, f32[2,4,8,128]{3,2,1,0:T(8,128)S(1)}, u32[]{:S(2)}) copy-start(f32[2,4,8,128]{3,2,1,0:T(8,128)S(1)} %reduce_window_sum.33) | copy-start | bytes 98308
  39.5 788.8 %copy-start.74 = (f32[2,4,8,128]{3,2,1,0:T(8,128)}, f32[2,4,8,128]{3,2,1,0:T(8,128)S(1)}, u32[]{:S(2)}) copy-start(f32[2,4,8,128]{3,2,1,0:T(8,128)S(1)} %exponential_multiply_fusion) | copy-start | bytes 98308
  724.8 21.5 %copy-start.70 = (f32[2,4,8,1,128]{4,3,2,1,0:T(1,128)}, f32[2,4,8,1,128]{4,3,2,1,0:T(1,128)S(1)}, u32[]{:S(2)}) copy-start(f32[2,4,8,1,128]{4,3,2,1,0:T(1,128)S(1)} %slice.153) | copy-start | bytes 98308
  724.8 11.9 copy-start.7
  825.9 97.3 %all-gather.11.cloned.1.call-start = ((), (), s32[]{:S(2)}) async-start(), calls=%async_computation.13 | async-start | bytes 4718592 | tf_op jit(solution)/shard_map/all_gather | solution.py:29
  828.2 384.8 %all-gather.13.cloned.1.call-start = ((), (), s32[]{:S(2)}) async-start(), calls=%async_computation.14 | async-start | bytes 4718592 | tf_op jit(solution)/shard_map/all_gather | solution.py:52
  857.4 355.7 %all-gather.15.cloned.1.call-start = ((), (), s32[]{:S(2)}) async-start(), calls=%async_computation.15 | async-start | bytes 4718592 | tf_op jit(solution)/shard_map/all_gather | solution.py:52
  1011.6 16.1 slice-start.4
  1014.3 13.4 copy-start.80
  1014.3 13.4 slice-start.5
  1063.0 12.0 slice-start
  1067.9 14.8 copy-start.25
  1093.9 452.6 %reduce-scatter.16.cloned.1.call-start = ((), (), s32[]{:S(2)}) async-start(), calls=%async_computation.9 | async-start | bytes 2359296 | tf_op jit(solution)/shard_map/reduce_scatter | solution.py:363
  1097.8 448.7 %reduce-scatter.14.cloned.1.call-start = ((), (), s32[]{:S(2)}) async-start(), calls=%async_computation.8 | async-start | bytes 2359296 | tf_op jit(solution)/shard_map/reduce_scatter | solution.py:363
  1101.9 444.7 %reduce-scatter.20.cloned.1.call-start = ((), (), s32[]{:S(2)}) async-start(), calls=%async_computation.11 | async-start | bytes 6488064 | tf_op jit(solution)/shard_map/reduce_scatter | solution.py:363
  1108.9 437.7 %reduce-scatter.18.cloned.1.call-start = ((), (), s32[]{:S(2)}) async-start(), calls=%async_computation.10 | async-start | bytes 12976128 | tf_op jit(solution)/shard_map/reduce_scatter | solution.py:363
  1109.1 13.3 copy-start.8
  1109.1 13.3 copy-start.35
  1122.4 11.8 copy-start.41
  1180.1 453.5 %reduce-scatter.12.cloned.1.call-start = ((), (), s32[]{:S(2)}) async-start(), calls=%async_computation.7 | async-start | bytes 11796480 | tf_op jit(solution)/shard_map/reduce_scatter | solution.py:363
  1329.6 11.5 copy-start.9
  1329.6 11.5 copy-start.19
  1329.6 11.5 copy-start.29
  1329.6 11.6 copy-start.71
  1341.2 16.4 slice-start.2
  1363.7 16.7 copy-start.27
  1380.4 11.3 copy-start.83
  1456.0 24.1 %copy-start.95 = (f32[5120,1]{0,1:T(1,128)S(1)}, f32[5120,1]{0,1:T(1,128)}, u32[]{:S(2)}) copy-start(f32[5120,1]{0,1:T(1,128)} %copy-done.94) | copy-start | bytes 61444
  1456.0 24.1 %copy-start.97 = (f32[5120,1]{0,1:T(1,128)S(1)}, f32[5120,1]{0,1:T(1,128)}, u32[]{:S(2)}) copy-start(f32[5120,1]{0,1:T(1,128)} %copy-done.96) | copy-start | bytes 61444
  1456.0 24.0 %copy-start.99 = (f32[5120,1]{0,1:T(1,128)S(1)}, f32[5120,1]{0,1:T(1,128)}, u32[]{:S(2)}) copy-start(f32[5120,1]{0,1:T(1,128)} %get-tuple-element.807) | copy-start | bytes 61444
  1456.0 24.0 %copy-start.101 = (f32[5120,1]{0,1:T(1,128)S(1)}, f32[5120,1]{0,1:T(1,128)}, u32[]{:S(2)}) copy-start(f32[5120,1]{0,1:T(1,128)} %get-tuple-element.808) | copy-start | bytes 61444
  1495.5 18.6 %copy-start.63 = (bf16[2,256,1024]{2,1,0:T(8,128)(2,1)S(1)}, bf16[2,256,1024]{2,1,0:T(8,128)(2,1)}, u32[]{:S(2)}) copy-start(bf16[2,256,1024]{2,1,0:T(8,128)(2,1)} %param.23) | copy-start | bytes 3145732
  1495.5 18.6 %copy-start.118 = (f32[1024]{0:T(1024)S(1)}, f32[1024]{0:T(1024)}, u32[]{:S(2)}) copy-start(f32[1024]{0:T(1024)} %copy-done.116) | copy-start | bytes 12292
  1495.5 18.6 %copy-start.121 = (f32[2,256]{1,0:T(2,128)S(1)}, f32[2,256]{1,0:T(2,128)}, u32[]{:S(2)}) copy-start(f32[2,256]{1,0:T(2,128)} %copy-done.119) | copy-start | bytes 6148
  1510.2 3.2 collective-permute-start.1
  1522.9 194.6 %reduce-scatter.22.cloned.1.call-start = ((), (), s32[]{:S(2)}) async-start(), calls=%async_computation.16 | async-start | bytes 1474560
  1527.4 14.5 copy-start.104
  1527.5 16.0 copy-start.93
  1527.5 16.0 copy-start.122
  1527.5 16.0 copy-start.124
  1543.8 174.8 %reduce-scatter.24.cloned.1.call-start = ((), (), s32[]{:S(2)}) async-start(), calls=%async_computation.17 | async-start | bytes 294912
  1545.2 259.6 %all-reduce.31.cloned.1.call-start = ((), (), s32[]{:S(2)}) async-start(), calls=%async_computation.18 | async-start | bytes 7995392 | tf_op jit(solution)/shard_map/psum | solution.py:367
  1638.4 45.3 %copy-start.105 = (bf16[1024,24]{0,1:T(8,128)(2,1)S(1)}, bf16[1024,24]{0,1:T(8,128)(2,1)}, u32[]{:S(2)}) copy-start(bf16[1024,24]{0,1:T(8,128)(2,1)} %param.28) | copy-start | bytes 147460
  1638.4 47.0 %copy-start.132 = (bf16[2,3,5120]{2,1,0:T(4,128)(2,1)S(1)}, bf16[2,3,5120]{2,1,0:T(4,128)(2,1)}, u32[]{:S(2)}) copy-start(bf16[2,3,5120]{2,1,0:T(4,128)(2,1)} %copy-done.131) | copy-start | bytes 184324
  1685.4 14.0 copy-start.126
  1685.4 29.0 %copy-start.115 = (f32[2,256]{1,0:T(2,128)S(1)}, f32[2,256]{1,0:T(2,128)}, u32[]{:S(2)}) copy-start(f32[2,256]{1,0:T(2,128)} %copy-done.114) | copy-start | bytes 6148
  1685.4 29.0 %copy-start.53 = (f32[2,256,1024]{2,1,0:T(8,128)S(1)}, f32[2,256,1024]{2,1,0:T(8,128)}, u32[]{:S(2)}) copy-start(f32[2,256,1024]{2,1,0:T(8,128)} %copy-done.51) | copy-start | bytes 6291460
  (103 other events, 544.7 us)
Sparse Core Ops, SparseCore 0:
  826.0 49.1 all-gather.8
  877.3 45.8 all-gather.10
  924.8 45.8 all-gather.12
  1094.0 45.7 all-gather.14
  1142.0 34.4 reduce-scatter.15
  1178.7 34.5 reduce-scatter.13
  1215.5 63.3 reduce-scatter.19
  1281.2 117.6 reduce-scatter.17
  1523.0 110.5 reduce-scatter.11
  1636.3 31.8 reduce-scatter.21
  1671.1 28.3 reduce-scatter.23
  1704.2 100.6 all-reduce.30
where the time goes:
time: 1830 us; the launch traced here: 1820 us
  other arithmetic  796 us (43%)
  matrix products  473 us (26%)
  local copies, waits for them, and re-layouts  236 us (13%)
  waiting for transfers between devices  223 us (12%)
  blocking collectives  68.8 us (4%)
    another operation x5, other arithmetic, block_maps(): jax.scipy.linalg.solve_triangular(mixing, right_side, lower=True, unit_di...  639 us
    dot_general x59, matrix products, full_product(): return jnp.einsum(formula, former, latter, precision=HIGHEST)  267 us
    dot_general x24, matrix products, half_product(): jnp.einsum(formula, former, latter, preferred_element_type=jnp.float32)  150 us
    reduce_scatter x5, waiting for transfers between devices, local(): lax.psum_scatter(shortened(mlp_terms + mixer_terms), 'seq', scatter_dimen...  87.1 us
    psum x1, waiting for transfers between devices, local(): lax.psum(shortened(shards), 'row')  67.5 us
    all_gather x2, waiting for transfers between devices, prefix(): lax.all_gather(part.astype(kind), axis)  65.8 us
    another operation x3, matrix products, block_maps(): jax.scipy.linalg.solve_triangular(mixing, right_side, lower=True, unit_di...  38.3 us
    psum x1, blocking collectives, local(): lax.psum((small_terms[0], small_terms[1], small_terms[2]), ('row', 'seq'))  38.3 us
  transfers between devices with their start and end apart: 14, of which 5 were waited for; matrix products, arithmetic and copies ran while one was open for 37% of the time, Pallas kernels for 0%

commit v1 on v0

v1 whole, which is shorter than its diff:
```python
from functools import partial

import jax
import jax.numpy as jnp
from jax import lax
from jax.experimental import pallas as pl
from jax.experimental.pallas import tpu as pltpu
from jax.sharding import PartitionSpec as P

D = 1024
HEADS = 8
HDIM = 128
NH = 2
FF = 2816
CHUNK = 128
VIRT = NH * CHUNK
GROUPS = 1 + 2 * NH
EPSILON = 1e-06
F32 = jnp.float32
BF16 = jnp.bfloat16
HIGHEST = lax.Precision.HIGHEST
VMEM_LIMIT = 48 * 1024 * 1024


def mm(former, latter, over=(1, 0)):
    return lax.dot_general(
        former.astype(BF16),
        latter.astype(BF16),
        (((over[0],), (over[1],)), ((), ())),
        preferred_element_type=F32,
    )


def exact_mm(former, latter):
    return jnp.dot(former, latter, precision=HIGHEST, preferred_element_type=F32)


def sigmoid(tensor):
    return 1.0 / (1.0 + jnp.exp(-tensor))


def iota2(shape, dim):
    return lax.broadcasted_iota(jnp.int32, shape, dim)


def params(*semantics):
    return pltpu.CompilerParams(
        dimension_semantics=semantics or None, vmem_limit_bytes=VMEM_LIMIT
    )


def front_kernel(x_ref, gain_ref, w_ref, lanes_ref, flags_ref, normed_ref, col_ref, row_ref):
    x = x_ref[0].astype(F32)
    length = x.shape[0]
    scale = lax.rsqrt(jnp.mean(x * x, axis=-1, keepdims=True) + EPSILON)
    normed = (x * scale * gain_ref[...]).astype(BF16)
    normed_ref[0] = normed
    rates = jnp.dot(normed, w_ref[...], preferred_element_type=F32)
    shifted = rates + lanes_ref[1:2]
    soft = jnp.maximum(shifted, 0.0) + jnp.log(1.0 + jnp.exp(-jnp.abs(shifted)))
    log_decay = lanes_ref[0:1] * soft
    shape = (length, length)
    here, there = iota2(shape, 0), iota2(shape, 1)
    lower = ((here >= there) & (here // CHUNK == there // CHUNK)).astype(F32)
    summed = exact_mm(lower, log_decay)
    last = jnp.concatenate(
        [
            jnp.broadcast_to(summed[at + CHUNK - 1 : at + CHUNK], (CHUNK, HDIM))
            for at in range(0, length, CHUNK)
        ],
        axis=0,
    )
    flags = flags_ref[0]
    start = jnp.exp(summed) * flags[:, 0:1]
    tail = jnp.exp(last - summed) * flags[:, 1:2]
    lane = iota2((length, HDIM), 1)
    packed = jnp.zeros((length, HDIM), F32)
    for limit, member, shift in (
        (56, log_decay, 32),
        (48, sigmoid(shifted), 24),
        (40, tail, 16),
        (32, start, 8),
        (24, summed, 0),
        (16, sigmoid(rates), 0),
    ):
        member = pltpu.roll(member, shift, 1) if shift else member
        packed = jnp.where(lane < limit, member, packed)
    col_ref[0] = packed
    row_ref[0] = packed.T


def front(hidden_in, gain, w_rates, a_log, dt_bias, flags):
    rows, length = hidden_in.shape[:2]
    w_padded = jnp.pad(w_rates, ((0, 0), (0, HDIM - w_rates.shape[1])))
    first = NH * HEADS
    lanes = jnp.pad(
        jnp.stack([-jnp.exp(a_log), dt_bias]), ((0, 0), (first, HDIM - first - HEADS))
    )
    return pl.pallas_call(
        front_kernel,
        grid=(rows,),
        in_specs=[
            pl.BlockSpec((1, length, D), lambda r: (r, 0, 0)),
            pl.BlockSpec((1, D), lambda r: (0, 0)),
            pl.BlockSpec((D, HDIM), lambda r: (0, 0)),
            pl.BlockSpec((2, HDIM), lambda r: (0, 0)),
            pl.BlockSpec((1, length, 2), lambda r: (r, 0, 0)),
        ],
        out_specs=[
            pl.BlockSpec((1, length, D), lambda r: (r, 0, 0)),
            pl.BlockSpec((1, length, HDIM), lambda r: (r, 0, 0)),
            pl.BlockSpec((1, HDIM, length), lambda r: (r, 0, 0)),
        ],
        out_shape=[
            jax.ShapeDtypeStruct((rows, length, D), BF16),
            jax.ShapeDtypeStruct((rows, length, HDIM), F32),
            jax.ShapeDtypeStruct((rows, HDIM, length), F32),
        ],
        compiler_params=params("arbitrary"),
        name="front",
    )(hidden_in, gain.astype(F32)[None], w_padded, lanes, flags)


def convolved(x_ref, halo_ref, taps_ref, keep_ref, ext_ref):
    length = x_ref.shape[1]
    ext_ref[0:8] = halo_ref[0].astype(F32)
    x = x_ref[0].astype(F32)
    ext_ref[8 : 8 + length] = x
    summed = x * taps_ref[3:4]
    for tap in range(3):
        summed = summed + ext_ref[5 + tap : 5 + tap + length] * keep_ref[0, tap] * taps_ref[
            tap : tap + 1
        ]
    return summed


def head_columns(col_ref, head):
    return pltpu.roll(col_ref[0], (HDIM - head) % HDIM, 1)


def both(tensor):
    return jnp.concatenate([tensor, tensor], axis=0)


def decay_matrix(cols, row_ref, mask_ref, head, chunk):
    at = chunk * CHUNK
    own = iota2((HEADS, CHUNK), 0) == head
    across = row_ref[0, 16:24, at : at + CHUNK]
    across = jnp.sum(jnp.where(own, across, 0.0), axis=0, keepdims=True)
    down = cols[at : at + CHUNK, 16:17]
    return jnp.exp(down - across + mask_ref[0, chunk])


def maps_kernel(*refs):
    xs, halos, taps = refs[0:5], refs[5:10], refs[10:15]
    keep_ref, col_ref, row_ref, mask_ref, level_ref = refs[15:20]
    q_ref, k_ref, v_ref, t_ref, wu_ref, p_ref, m_ref, dev_ref, ext_ref = refs[20:]
    head = pl.program_id(1)
    length = xs[0].shape[1]
    chunks = length // CHUNK
    cols = head_columns(col_ref, head)
    parts = []
    for group in range(GROUPS):
        summed = convolved(
            xs[group], halos[group], taps[group], keep_ref, ext_ref.at[group]
        )
        active = summed * sigmoid(summed)
        if group < 1 + NH:
            active = active * lax.rsqrt(
                jnp.sum(active * active, axis=-1, keepdims=True) + EPSILON
            )
        parts.append(active.astype(BF16))
    q_ref[0, 0] = parts[0]
    level = level_ref[...]
    eye = (iota2((HDIM, HDIM), 0) == iota2((HDIM, HDIM), 1)).astype(F32)
    eye_wide = (iota2((VIRT, VIRT), 0) == iota2((VIRT, VIRT), 1)).astype(F32)
    data = []
    for chunk in range(chunks):
        at = chunk * CHUNK
        rows = slice(at, at + CHUNK)
        query = parts[0][rows]
        keys = jnp.concatenate([parts[1][rows], parts[2][rows]], axis=0)
        values = jnp.concatenate([parts[3][rows], parts[4][rows]], axis=0)
        k_ref[0, 0, chunk] = keys
        v_ref[0, 0, chunk] = values
        decay = decay_matrix(cols, row_ref, mask_ref, head, chunk)
        wide_decay = jnp.concatenate([decay, decay], axis=1)
        beta = jnp.concatenate([cols[rows, 0:1], cols[rows, 8:9]], axis=0)
        mixing = (mm(keys, keys, (1, 1)) * both(wide_decay) * beta).astype(BF16).astype(F32)
        p_ref[0, 0, chunk] = (mm(query, keys, (1, 1)) * wide_decay).astype(BF16)
        inverse = (eye_wide - jnp.where(level == 0, mixing, 0.0)).astype(BF16)
        data.append((keys, values, beta, mixing, inverse))
    for step in range(1, 8):
        mids = [
            mm(jnp.where(level == step, mixing, 0.0), inverse)
            for keys, values, beta, mixing, inverse in data
        ]
        data = [
            (keys, values, beta, mixing, inverse - mm(inverse, mid).astype(BF16))
            for (keys, values, beta, mixing, inverse), mid in zip(data, mids)
        ]
    device_m, device_b = None, None
    for chunk, (keys, values, beta, mixing, inverse) in enumerate(data):
        at = chunk * CHUNK
        rows = slice(at, at + CHUNK)
        t_ref[0, 0, chunk] = inverse
        keys_float = keys.astype(F32)
        right = jnp.concatenate(
            [keys_float * (both(cols[rows, 24:25]) * beta), values.astype(F32) * beta], axis=1
        )
        solved = mm(inverse, right).astype(BF16)
        wu_ref[0, 0, chunk] = solved
        tail_keys = keys_float * both(cols[rows, 32:33])
        pair = mm(solved, tail_keys, (0, 0))
        block_m = cols[at + CHUNK - 1 : at + CHUNK, 24:25] * eye - pair[:HDIM]
        block_b = pair[HDIM:]
        m_ref[0, 0, chunk] = block_m.astype(BF16)
        if device_m is None:
            device_m, device_b = block_m, block_b
        else:
            chained = mm(jnp.concatenate([device_m, device_b], axis=0), block_m)
            device_m, device_b = chained[:HDIM], chained[HDIM:] + block_b
    dev_ref[0, 0, 0] = device_m.astype(BF16)
    dev_ref[1, 0, 0] = device_b.astype(BF16)


def group_specs(block, index):
    return [
        pl.BlockSpec(block, partial(lambda g, r, h: index(r, g * HEADS + h), g))
        for g in range(GROUPS)
    ]


def head_spec(*block):
    return pl.BlockSpec(
        (1, 1) + block, lambda r, h: (r, h) + (0,) * len(block)
    )


def conv_specs(length):
    return (
        group_specs((1, length, HDIM), lambda r, c: (r, 0, c))
        + group_specs((1, 8, HDIM), lambda r, c: (r, 0, c))
        + group_specs((4, HDIM), lambda r, c: (0, c))
        + [pl.BlockSpec((1, 3, length, HDIM), lambda r, h: (r, 0, 0, 0))]
    )


def rate_specs(length):
    return [
        pl.BlockSpec((1, length, HDIM), lambda r, h: (r, 0, 0)),
        pl.BlockSpec((1, HDIM, length), lambda r, h: (r, 0, 0)),
        pl.BlockSpec((1, length // CHUNK, CHUNK, CHUNK), lambda r, h: (r, 0, 0, 0)),
    ]


def levels():
    place = jnp.arange(VIRT)
    place = NH * (place % CHUNK) + place // CHUNK
    differ = place[:, None] ^ place[None, :]
    level = sum((differ >= (1 << bit)).astype(jnp.int32) for bit in range(1, 8))
    return jnp.where(place[:, None] > place[None, :], level, -1)


def maps(projected, halo, taps, keep, col, row, mask, level):
    rows, length = projected.shape[:2]
    chunks = length // CHUNK
    shape = lambda *tail: jax.ShapeDtypeStruct((rows, HEADS) + tail, BF16)
    wide = pl.BlockSpec((VIRT, VIRT), lambda r, h: (0, 0))
    return pl.pallas_call(
        maps_kernel,
        grid=(rows, HEADS),
        in_specs=conv_specs(length) + rate_specs(length) + [wide],
        out_specs=[
            head_spec(length, HDIM),
            head_spec(chunks, VIRT, HDIM),
            head_spec(chunks, VIRT, HDIM),
            head_spec(chunks, VIRT, VIRT),
            head_spec(chunks, VIRT, VIRT),
            head_spec(chunks, CHUNK, VIRT),
            head_spec(chunks, HDIM, HDIM),
            pl.BlockSpec((2, 1, 1, HDIM, HDIM), lambda r, h: (0, r, h, 0, 0)),
        ],
        out_shape=[
            shape(length, HDIM),
            shape(chunks, VIRT, HDIM),
            shape(chunks, VIRT, HDIM),
            shape(chunks, VIRT, VIRT),
            shape(chunks, VIRT, VIRT),
            shape(chunks, CHUNK, VIRT),
            shape(chunks, HDIM, HDIM),
            jax.ShapeDtypeStruct((2, rows, HEADS, HDIM, HDIM), BF16),
        ],
        scratch_shapes=[pltpu.VMEM((GROUPS, length + 8, HDIM), F32)],
        compiler_params=params("arbitrary", "arbitrary"),
        name="maps",
    )(*([projected] * 5 + [halo] * 5 + [taps] * 5), keep, col, row, mask, level)


def mixed_kernel(
    q_ref, k_ref, wu_ref, p_ref, col_ref, state_ref, gate_ref, gain_ref,
    branch_ref, mixed_ref, states_ref, delta_ref,
):
    head = pl.program_id(1)
    cols = head_columns(col_ref, head)
    state = state_ref[0, 0].astype(F32)
    chunks = k_ref.shape[2]
    outputs = []
    for chunk in range(chunks):
        at = chunk * CHUNK
        rows = slice(at, at + CHUNK)
        solved = wu_ref[0, 0, chunk]
        states_ref[0, 0, chunk] = state.astype(BF16)
        seen = mm(
            jnp.concatenate([solved[:, :HDIM], q_ref[0, 0, rows]], axis=0), state, (1, 1)
        )
        delta = (solved[:, HDIM:].astype(F32) - seen[:VIRT]).astype(BF16)
        delta_ref[0, 0, chunk] = delta
        outputs.append(cols[rows, 24:25] * seen[VIRT:] + mm(p_ref[0, 0, chunk], delta))
        if chunk + 1 < chunks:
            tail_keys = k_ref[0, 0, chunk].astype(F32) * both(cols[rows, 32:33])
            state = cols[at + CHUNK - 1 : at + CHUNK, 24:25] * state + mm(
                delta, tail_keys, (0, 0)
            )
    mixed = jnp.concatenate(outputs, axis=0)
    mixed_ref[0] = mixed
    scale = lax.rsqrt(jnp.mean(mixed * mixed, axis=-1, keepdims=True) + EPSILON)
    gate = gate_ref[0]
    branch_ref[0] = (mixed * scale * gain_ref[...] * (gate * sigmoid(gate))).astype(BF16)


def column_spec(length):
    return pl.BlockSpec((1, length, HDIM), lambda r, h: (r, 0, h))


def mix(q, k, wu, p, col, state_in, gate, gain):
    rows, _, length = q.shape[:3]
    chunks = length // CHUNK
    return pl.pallas_call(
        mixed_kernel,
        grid=(rows, HEADS),
        in_specs=[
            head_spec(length, HDIM),
            head_spec(chunks, VIRT, HDIM),
            head_spec(chunks, VIRT, VIRT),
            head_spec(chunks, CHUNK, VIRT),
            rate_specs(length)[0],
            head_spec(HDIM, HDIM),
            column_spec(length),
            pl.BlockSpec((1, HDIM), lambda r, h: (0, 0)),
        ],
        out_specs=[
            column_spec(length),
            column_spec(length),
            head_spec(chunks, HDIM, HDIM),
            head_spec(chunks, VIRT, HDIM),
        ],
        out_shape=[
            jax.ShapeDtypeStruct((rows, length, D), BF16),
            jax.ShapeDtypeStruct((rows, length, D), F32),
            jax.ShapeDtypeStruct((rows, HEADS, chunks, HDIM, HDIM), BF16),
            jax.ShapeDtypeStruct((rows, HEADS, chunks, VIRT, HDIM), BF16),
        ],
        compiler_params=params("arbitrary", "arbitrary"),
        name="mix",
    )(q, k, wu, p, col, state_in, gate, gain.astype(F32)[None])


def adjoint_kernel(
    up_ref, mixed_ref, gate_ref, gain_ref, q_ref, wu_ref, p_ref, m_ref, col_ref,
    grad_mixed_ref, grad_gate_ref, grad_gain_ref, own_ref,
):
    head = pl.program_id(1)
    cols = head_columns(col_ref, head)
    chunks = p_ref.shape[2]
    upstream, mixed, gate, gain = up_ref[0], mixed_ref[0], gate_ref[0], gain_ref[...]
    sig = sigmoid(gate)
    scale = lax.rsqrt(jnp.mean(mixed * mixed, axis=-1, keepdims=True) + EPSILON)
    unit = mixed * scale
    grad_gate_ref[0] = (
        upstream * unit * gain * (sig * (1.0 + gate * (1.0 - sig)))
    ).astype(BF16)
    upstream = upstream * (gate * sig)
    partial_gain = upstream * unit
    grad_gain_ref[0, 0] = jnp.sum(
        partial_gain.reshape(partial_gain.shape[0] // 8, 8, HDIM), axis=0
    )
    weighted = gain * upstream
    grad_mixed = scale * (weighted - unit * jnp.mean(unit * weighted, axis=-1, keepdims=True))
    low = grad_mixed.astype(BF16)
    grad_mixed_ref[0] = low
    grad_state = None
    for chunk in reversed(range(chunks)):
        at = chunk * CHUNK
        rows = slice(at, at + CHUNK)
        own_delta = mm(p_ref[0, 0, chunk], low[rows], (0, 0))
        left = jnp.concatenate(
            [(grad_mixed[rows] * cols[rows, 24:25]).astype(BF16), (-own_delta).astype(BF16)],
            axis=0,
        )
        right = jnp.concatenate([q_ref[0, 0, rows], wu_ref[0, 0, chunk, :, :HDIM]], axis=0)
        own = mm(left, right, (0, 0))
        if grad_state is not None:
            own = own + mm(grad_state, m_ref[0, 0, chunk], (1, 1))
        grad_state = own
    own_ref[0, 0] = grad_state.astype(BF16)


def adjoint(upstream, mixed, gate, gain, q, wu, p, m, col):
    rows, _, length = q.shape[:3]
    chunks = length // CHUNK
    return pl.pallas_call(
        adjoint_kernel,
        grid=(rows, HEADS),
        in_specs=[
            column_spec(length),
            column_spec(length),
            column_spec(length),
            pl.BlockSpec((1, HDIM), lambda r, h: (0, 0)),
            head_spec(length, HDIM),
            head_spec(chunks, VIRT, VIRT),
            head_spec(chunks, CHUNK, VIRT),
            head_spec(chunks, HDIM, HDIM),
            rate_specs(length)[0],
        ],
        out_specs=[
            column_spec(length),
            column_spec(length),
            head_spec(8, HDIM),
            head_spec(HDIM, HDIM),
        ],
        out_shape=[
            jax.ShapeDtypeStruct((rows, length, D), BF16),
            jax.ShapeDtypeStruct((rows, length, D), BF16),
            jax.ShapeDtypeStruct((rows, HEADS, 8, HDIM), F32),
            jax.ShapeDtypeStruct((rows, HEADS, HDIM, HDIM), BF16),
        ],
        compiler_params=params("arbitrary", "arbitrary"),
        name="adjoint",
    )(upstream, mixed, gate, gain.astype(F32)[None], q, wu, p, m, col)


def back_kernel(*refs):
    xs, halos, taps = refs[0:5], refs[5:10], refs[10:15]
    keep_ref, col_ref, row_ref, mask_ref, level_ref = refs[15:20]
    q_ref, k_ref, v_ref, t_ref, wu_ref, p_ref, states_ref, delta_ref = refs[20:28]
    grad_mixed_ref, state_ref = refs[28:30]
    gp_ref, gh_ref, gw_ref, stats_ref, ext_ref, shift_ref = refs[30:]
    head = pl.program_id(1)
    length = xs[0].shape[1]
    chunks = length // CHUNK
    cols = head_columns(col_ref, head)
    strict = level_ref[...] >= 0
    lane = iota2((CHUNK, CHUNK), 1)
    last_row = iota2((CHUNK, 1), 0) == CHUNK - 1
    own_row = iota2((HEADS, CHUNK), 0) == head
    grad_next = state_ref[0, 0].astype(F32)
    grads = [[None] * chunks for _ in range(GROUPS)]
    for chunk in reversed(range(chunks)):
        at = chunk * CHUNK
        rows = slice(at, at + CHUNK)
        query = q_ref[0, 0, rows]
        query_float = query.astype(F32)
        keys, values = k_ref[0, 0, chunk], v_ref[0, 0, chunk]
        keys_float, values_float = keys.astype(F32), values.astype(F32)
        solved, scores = wu_ref[0, 0, chunk], p_ref[0, 0, chunk]
        state, delta = states_ref[0, 0, chunk], delta_ref[0, 0, chunk]
        grad_out = grad_mixed_ref[0, rows]
        beta = jnp.concatenate([cols[rows, 0:1], cols[rows, 8:9]], axis=0)
        start, tail = cols[rows, 24:25], cols[rows, 32:33]
        start_wide, tail_wide = both(start), both(tail)
        end = cols[at + CHUNK - 1 : at + CHUNK, 24:25]
        decay = decay_matrix(cols, row_ref, mask_ref, head, chunk)
        wide_decay = jnp.concatenate([decay, decay], axis=1)
        full_decay = jnp.where(strict, both(wide_decay), 0.0)
        next_low = grad_next.astype(BF16)
        tail_keys = (keys_float * tail_wide).astype(BF16)
        grad_delta = mm(scores, grad_out, (0, 0)) + mm(tail_keys, next_low, (1, 1))
        delta_low = grad_delta.astype(BF16)
        grad_scores = mm(grad_out, delta, (1, 1))
        weighted_scores = grad_scores * scores.astype(F32)
        grad_raw = (grad_scores * wide_decay).astype(BF16)
        seen = mm(jnp.concatenate([grad_out, delta_low], axis=0), state)
        grad_query = start * seen[:CHUNK] + mm(grad_raw, keys)
        grad_start = jnp.sum(seen[:CHUNK] * query_float, axis=1, keepdims=True)
        grad_wide = jnp.concatenate([-seen[CHUNK:], grad_delta], axis=1).astype(BF16)
        grad_end = jnp.sum(
            jnp.sum(grad_next * state.astype(F32), axis=1, keepdims=True), axis=0, keepdims=True
        )
        grad_tail_keys = mm(delta, next_low)
        left = jnp.concatenate(
            [(grad_out.astype(F32) * start).astype(BF16), (-grad_delta).astype(BF16)], axis=0
        )
        grad_next = end * grad_next + mm(
            left, jnp.concatenate([query, solved[:, :HDIM]], axis=0), (0, 0)
        )
        grad_right = mm(t_ref[0, 0, chunk], grad_wide, (0, 0))
        right_keys, right_values = grad_right[:, :HDIM], grad_right[:, HDIM:]
        grad_mixing = -mm(grad_right, solved, (1, 1))
        gram = mm(keys, keys, (1, 1))
        decayed = grad_mixing * full_decay
        weighted = decayed * gram
        grad_gram = (decayed * beta).astype(BF16)
        by_keys = jnp.sum(keys_float * right_keys, axis=1, keepdims=True)
        by_values = jnp.sum(values_float * right_values, axis=1, keepdims=True)
        by_mixing = jnp.sum(weighted, axis=1, keepdims=True)
        grad_beta = start_wide * by_keys + by_values + by_mixing
        grad_keys = (
            (start_wide * beta) * right_keys
            + tail_wide * grad_tail_keys
            + mm(grad_raw, query, (0, 0))
            + mm(grad_gram, keys)
            + mm(grad_gram, keys, (0, 0))
        )
        grad_values = beta * right_values
        fold = lambda tensor: tensor[:CHUNK] + tensor[CHUNK:]
        across = jnp.sum(beta * weighted, axis=0, keepdims=True) + jnp.sum(
            weighted_scores, axis=0, keepdims=True
        )
        across = across[:, :CHUNK] + across[:, CHUNK:]
        tail_part = (
            fold(jnp.sum(keys_float * grad_tail_keys, axis=1, keepdims=True)) * tail
        )
        down = (
            fold(beta * by_mixing)
            + jnp.sum(weighted_scores, axis=1, keepdims=True)
            + (grad_start + fold(beta * by_keys)) * start
            - tail_part
        )
        at_end = jnp.sum(tail_part, axis=0, keepdims=True) + grad_end * end
        down = down + jnp.where(last_row, at_end, 0.0)
        columns = jnp.where(
            lane == 0, grad_beta[:CHUNK], jnp.where(lane == 1, grad_beta[CHUNK:], down)
        )
        turned = columns.T
        for place, member in enumerate((turned[0:1], turned[1:2], turned[2:3] - across)):
            spot = slice(place * HEADS, place * HEADS + HEADS)
            stats_ref[0, spot, rows] = jnp.where(own_row, member, stats_ref[0, spot, rows])
        for group, member in enumerate(
            (grad_query, grad_keys[:CHUNK], grad_keys[CHUNK:], grad_values[:CHUNK], grad_values[CHUNK:])
        ):
            grads[group][chunk] = member
    for tap in range(3):
        shift_ref[tap, 0:8] = jnp.zeros((8, HDIM), F32)
        shift_ref[tap, 8 + length : 16 + length] = jnp.zeros((8, HDIM), F32)
    for group in range(GROUPS):
        ext = ext_ref.at[group]
        summed = convolved(xs[group], halos[group], taps[group], keep_ref, ext)
        sig = sigmoid(summed)
        active = summed * sig
        grad = jnp.concatenate(grads[group], axis=0).astype(BF16).astype(F32)
        if group < 1 + NH:
            scale = lax.rsqrt(jnp.sum(active * active, axis=-1, keepdims=True) + EPSILON)
            unit = active * scale
            grad = scale * (grad - unit * jnp.sum(unit * grad, axis=-1, keepdims=True))
        grad = grad * (sig * (1.0 + summed * (1.0 - sig)))
        total = grad * taps[group][3:4]
        before = None
        weight_rows = []
        for tap in range(3):
            kept = grad * keep_ref[0, tap]
            weight_rows.append(
                jnp.sum(kept * ext[5 + tap : 5 + tap + length], axis=0, keepdims=True)
            )
            shift_ref[tap, 8 : 8 + length] = kept * taps[group][tap : tap + 1]
            total = total + shift_ref[tap, 11 - tap : 11 - tap + length]
            early = shift_ref[tap, 3 - tap : 11 - tap]
            before = early if before is None else before + early
        weight_rows.append(
            jnp.sum(grad * ext[8 : 8 + length], axis=0, keepdims=True)
        )
        gp_ref[group, 0] = total.astype(BF16)
        gh_ref[group, 0] = before.astype(BF16)
        gw_ref[0, group, 0] = jnp.concatenate(
            weight_rows + [jnp.zeros((4, HDIM), F32)], axis=0
        )


def back(projected, halo, taps, keep, col, row, mask, level, saved, grad_mixed, adjoint_in):
    rows, length = projected.shape[:2]
    chunks = length // CHUNK
    wide = pl.BlockSpec((VIRT, VIRT), lambda r, h: (0, 0))
    return pl.pallas_call(
        back_kernel,
        grid=(rows, HEADS),
        in_specs=conv_specs(length)
        + rate_specs(length)
        + [wide]
        + [
            head_spec(length, HDIM),
            head_spec(chunks, VIRT, HDIM),
            head_spec(chunks, VIRT, HDIM),
            head_spec(chunks, VIRT, VIRT),
            head_spec(chunks, VIRT, VIRT),
            head_spec(chunks, CHUNK, VIRT),
            head_spec(chunks, HDIM, HDIM),
            head_spec(chunks, VIRT, HDIM),
            column_spec(length),
            head_spec(HDIM, HDIM),
        ],
        out_specs=[
            pl.BlockSpec((GROUPS, 1, length, HDIM), lambda r, h: (0, r, 0, h)),
            pl.BlockSpec((GROUPS, 1, 8, HDIM), lambda r, h: (0, r, 0, h)),
            pl.BlockSpec((1, GROUPS, 1, 8, HDIM), lambda r, h: (r, 0, h, 0, 0)),
            pl.BlockSpec((1, 24, length), lambda r, h: (r, 0, 0)),
        ],
        out_shape=[
            jax.ShapeDtypeStruct((GROUPS, rows, length, D), BF16),
            jax.ShapeDtypeStruct((GROUPS, rows, 8, D), BF16),
            jax.ShapeDtypeStruct((rows, GROUPS, HEADS, 8, HDIM), F32),
            jax.ShapeDtypeStruct((rows, 24, length), F32),
        ],
        scratch_shapes=[
            pltpu.VMEM((GROUPS, length + 8, HDIM), F32),
            pltpu.VMEM((3, length + 16, HDIM), F32),
        ],
        compiler_params=params("arbitrary", "arbitrary"),
        name="back",
    )(
        *([projected] * 5 + [halo] * 5 + [taps] * 5),
        keep, col, row, mask, level, *saved, grad_mixed, adjoint_in,
    )


def rates_kernel(stats_ref, row_ref, nega_ref, rates_ref, sums_ref):
    rows, _, length = stats_ref.shape
    shape = (length, length)
    here, there = iota2(shape, 0), iota2(shape, 1)
    lower = ((here >= there) & (here // CHUNK == there // CHUNK)).astype(F32)
    lane = iota2((HEADS, HDIM), 1)
    total = jnp.zeros((HEADS, HDIM), F32)
    for r in range(rows):
        beta = row_ref[r, 0:16]
        grad_log = exact_mm(stats_ref[r, 16:24], lower)
        grad_bias = grad_log * nega_ref[:, 0:1] * row_ref[r, 40:48]
        rates_ref[r, 0:16] = (stats_ref[r, 0:16] * beta * (1.0 - beta)).astype(BF16)
        rates_ref[r, 16:24] = grad_bias.astype(BF16)
        rates_ref[r, 24:32] = jnp.zeros((8, length), BF16)
        by_log = jnp.sum(grad_log * row_ref[r, 48:56], axis=1, keepdims=True)
        by_bias = jnp.sum(grad_bias, axis=1, keepdims=True)
        total = total + jnp.where(lane == 0, by_log, jnp.where(lane == 1, by_bias, 0.0))
    sums_ref[...] = total


def rates_back(stats, row, a_log):
    rows, _, length = stats.shape
    nega = jnp.broadcast_to(-jnp.exp(a_log)[:, None], (HEADS, HDIM))
    return pl.pallas_call(
        rates_kernel,
        out_shape=[
            jax.ShapeDtypeStruct((rows, 32, length), BF16),
            jax.ShapeDtypeStruct((HEADS, HDIM), F32),
        ],
        compiler_params=params(),
        name="rates_back",
    )(stats, row, nega)


def to_core(value):
    count = lax.axis_size("seq")
    return lax.ppermute(value, "seq", [(at, at ^ 1) for at in range(count)])


def to_chip(value, step):
    count = lax.axis_size("seq")
    pairs = [(at, at + 2 * step) for at in range(count) if 0 <= at + 2 * step < count]
    return lax.ppermute(value, "seq", pairs)


def along(value, step):
    count = lax.axis_size("seq")
    pairs = [(at, at + step) for at in range(count) if 0 <= at + step < count]
    return lax.ppermute(value, "seq", pairs)


def chain(former, latter, transposed):
    formula = "rhva,rhba->rhvb" if transposed else "rhva,rhab->rhvb"
    return jnp.einsum(formula, former.astype(BF16), latter.astype(BF16), preferred_element_type=F32)


def carried(device_m, device_b, step):
    transposed = step < 0
    core = lax.axis_index("seq") % 2
    half = device_b.shape[0] // 2
    mine = lambda tensor, which: lax.dynamic_slice_in_dim(tensor, which * half, half, 0)
    own_m, own_b = mine(device_m, core), mine(device_b, core)
    other_m, other_b = to_core((mine(device_m, 1 - core), mine(device_b, 1 - core)))
    own_first = core == (0 if step > 0 else 1)
    first_m = jnp.where(own_first, own_m, other_m)
    first_b = jnp.where(own_first, own_b, other_b)
    second_m = jnp.where(own_first, other_m, own_m)
    second_b = jnp.where(own_first, other_b, own_b)
    if transposed:
        chip_m = chain(second_m, first_m, False).astype(BF16)
    else:
        chip_m = chain(first_m, second_m, False).astype(BF16)
    chip_b = chain(first_b, second_m, transposed) + second_b.astype(F32)
    leaving = chip_b.astype(BF16)
    entering = jnp.zeros_like(leaving)
    steps = lax.axis_size("seq") // 2 - 1
    for at in range(steps):
        entering = to_chip(leaving, step)
        if at + 1 < steps:
            leaving = (chain(entering, chip_m, transposed) + chip_b).astype(BF16)
    between = (chain(entering, first_m, transposed) + first_b.astype(F32)).astype(BF16)
    keep = jnp.where(own_first, entering, between)
    give = jnp.where(own_first, between, entering)
    got = to_core(give)
    low = jnp.where(core == 0, keep, got)
    high = jnp.where(core == 0, got, keep)
    return jnp.concatenate([low, high], axis=0)


def half_product(formula, former, latter):
    return jnp.einsum(formula, former, latter, preferred_element_type=F32)


def shortened(value):
    return jax.tree.map(lambda part: part.astype(BF16), value)


def rms_norm(tensor, gain):
    return tensor * lax.rsqrt(jnp.mean(tensor * tensor, axis=-1, keepdims=True) + EPSILON) * gain


def swiglu(gate_up):
    return jax.nn.silu(gate_up[..., :FF]) * gate_up[..., FF:]


def find_docs(doc_ends, places):
    found = jnp.sum((places[None, :, None] >= doc_ends[:, None, :]).astype(jnp.int32), axis=2)
    return jnp.where(places[None, :] >= 0, found, -1)


def doc_masks(lengths, length):
    anchor = lax.axis_index("seq") * length
    doc_ends = jnp.cumsum(lengths, axis=1)
    extended = find_docs(doc_ends, anchor + jnp.arange(-3, length, dtype=jnp.int32))
    docs = extended[:, 3:]
    rows = docs.shape[0]
    keep = jnp.stack([extended[:, tap : tap + length] == docs for tap in range(3)], axis=1)
    keep = jnp.broadcast_to(keep.astype(F32)[..., None], keep.shape + (HDIM,))
    chunks = length // CHUNK
    blocks = docs.reshape(rows, chunks, CHUNK)
    before = find_docs(doc_ends, anchor + jnp.arange(0, length, CHUNK, dtype=jnp.int32) - 1)
    carry = blocks == before[..., None]
    same_last = blocks == blocks[..., -1:]
    flags = jnp.stack([carry, same_last], axis=-1).astype(F32).reshape(rows, length, 2)
    places = jnp.arange(CHUNK)
    allowed = (blocks[..., :, None] == blocks[..., None, :]) & (places[:, None] >= places)
    return keep, flags, jnp.where(allowed, 0.0, -1e30).astype(F32)


def local(
    hidden_in, lengths, norm1_gain, w_qkv, conv_w, w_rates, a_log, dt_bias,
    w_gate, out_gain, w_out, norm2_gain, w_up, w_down, cotangent,
):
    row_count, length = hidden_in.shape[:2]
    keep, flags, mask = doc_masks(lengths, length)
    level = levels()
    taps = conv_w.astype(F32).T
    input_float = hidden_in.astype(F32)
    normed, col, row = front(hidden_in, norm1_gain, w_rates, a_log, dt_bias, flags)
    projected = half_product("rld,de->rle", normed, w_qkv).astype(BF16)
    halo = along(projected[:, length - 8 :], 1)
    q, k, v, t, wu, p, m, device = maps(projected, halo, taps, keep, col, row, mask, level)
    gate = half_product("rld,de->rle", normed, w_gate)
    state_in = carried(device[0], device[1], 1)
    branch, mixed, states, delta = mix(q, k, wu, p, col, state_in, gate, out_gain)
    hidden = input_float + half_product("rld,de->rle", branch, w_out)
    normed2_float, norm2_back = jax.vjp(rms_norm, hidden, norm2_gain.astype(F32))
    normed2 = normed2_float.astype(BF16)
    gate_up = half_product("rld,de->rle", normed2, w_up)
    activated_float, swiglu_back = jax.vjp(swiglu, gate_up)
    activated = activated_float.astype(BF16)
    layer_out = (hidden + half_product("rlf,fd->rld", activated, w_down)).astype(BF16)
    grad_w_down = half_product("rlf,rld->fd", activated, cotangent)
    grad_act = half_product("rld,fd->rlf", cotangent, w_down)
    grad_gate_up = swiglu_back(grad_act)[0].astype(BF16)
    grad_w_up = half_product("rld,rle->de", normed2, grad_gate_up)
    grad_normed2 = half_product("rle,de->rld", grad_gate_up, w_up)
    grad_hidden_part, grad_norm2_gain = norm2_back(grad_normed2)
    grad_hidden = cotangent.astype(F32) + grad_hidden_part
    grad_attended = grad_hidden.astype(BF16)
    grad_w_out = half_product("rld,rle->de", branch, grad_attended)
    grad_branch = half_product("rle,de->rld", grad_attended, w_out)
    grad_mixed, grad_gate, gain_parts, own = adjoint(
        grad_branch, mixed, gate, out_gain, q, wu, p, m, col
    )
    grad_out_gain = jnp.sum(gain_parts, axis=(0, 1, 2))
    adjoint_in = carried(device[0], own, -1)
    gp, gh, gw, stats = back(
        projected, halo, taps, keep, col, row, mask, level,
        (q, k, v, t, wu, p, states, delta), grad_mixed, adjoint_in,
    )
    returned = along(gh, -1)
    grad_projected = jnp.moveaxis(gp, 0, 2).reshape(row_count, length, GROUPS * D)
    returned = jnp.moveaxis(returned, 0, 2).reshape(row_count, 8, GROUPS * D)
    tail = (grad_projected[:, length - 8 :].astype(F32) + returned.astype(F32)).astype(BF16)
    grad_projected = lax.dynamic_update_slice_in_dim(grad_projected, tail, length - 8, 1)
    grad_conv_w = jnp.moveaxis(jnp.sum(gw, axis=0)[:, :, :4], 2, 3).reshape(GROUPS * D, 4)
    grad_rates, rate_sums = rates_back(stats, row, a_log)
    grad_rates = grad_rates[:, :24]
    grad_w_qkv = half_product("rld,rle->de", normed, grad_projected)
    grad_w_rates = half_product("rld,rel->de", normed, grad_rates)
    grad_w_gate = half_product("rld,rle->de", normed, grad_gate)
    grad_normed = half_product("rle,de->rld", grad_projected, w_qkv)
    grad_normed = grad_normed + half_product("rel,de->rld", grad_rates, w_rates)
    grad_normed = grad_normed + half_product("rle,de->rld", grad_gate, w_gate)
    _, norm1_back = jax.vjp(rms_norm, input_float, norm1_gain.astype(F32))
    grad_input_part, grad_norm1_gain = norm1_back(grad_normed)
    grad_x = (grad_hidden + grad_input_part).astype(BF16)
    mlp_terms = (grad_norm2_gain, grad_w_up, grad_w_down)
    mixer_terms = (grad_norm1_gain, grad_w_qkv, grad_conv_w, grad_w_rates, grad_w_gate, grad_w_out)
    small_sums = lax.psum((rate_sums[:, 0], rate_sums[:, 1], grad_out_gain), ("row", "seq"))
    shards = jax.tree.map(
        lambda part: part.astype(F32),
        lax.psum_scatter(
            shortened(mlp_terms + mixer_terms), "seq", scatter_dimension=0, tiled=True
        ),
    )
    totals = jax.tree.map(lambda part: part.astype(F32), lax.psum(shortened(shards), "row"))
    return (
        layer_out,
        grad_x,
        totals[3],
        totals[4],
        totals[5],
        totals[6],
        small_sums[0],
        small_sums[1],
        totals[7],
        small_sums[2],
        totals[8],
        totals[0],
        totals[1],
        totals[2],
    )


def solution(mesh):
    return jax.shard_map(
        local,
        mesh=mesh,
        in_specs=(
            P("row", "seq", None),
            P("row", None),
            P(),
            P(),
            P(),
            P(),
            P(),
            P(),
            P(),
            P(),
            P(),
            P(),
            P(),
            P(),
            P("row", "seq", None),
        ),
        out_specs=(
            P("row", "seq", None),
            P("row", "seq", None),
            P("seq"),
            P("seq", None),
            P("seq", None),
            P("seq", None),
            P(),
            P(),
            P("seq", None),
            P(),
            P("seq", None),
            P("seq"),
            P("seq", None),
            P("seq", None),
        ),
        check_vma=False,
    )
```

time: 1830 us -> 847 us (0.46)
  other arithmetic: 796 us -> 32.4 us
  matrix products: 473 us -> 130 us
  local copies, waits for them, and re-layouts: 236 us -> 73.5 us
  Pallas kernels: 0 us -> 162 us
  waiting for transfers between devices: 223 us -> 329 us
  starting transfers between devices: 5.5 us -> 24.2 us
    another operation x8 -> x3, other arithmetic: 652 us -> 2.24 us  [the longest x1 0.85 us: doc_masks(): doc_ends = jnp.cumsum(lengths, axis=1)]
    dot_general x84 -> x27, matrix products: 434 us -> 130 us  [the longest x17 121 us: half_product(): return jnp.einsum(formula, former, latter, preferred_element_type=F32)]
    pallas_call x0 -> x6, Pallas kernels: none -> 162 us  [the longest x1 68 us: maps(): pl.pallas_call(maps_kernel, grid=(rows, HEADS), in_specs=conv_specs(lengt...]
    reduce_scatter x5, waiting for transfers between devices: 87.1 us -> 204 us  [local(): lax.psum_scatter(shortened(mlp_terms + mixer_terms), 'seq', scatter_dimen...]
    dynamic_slice x48 -> x3, local copies, waits for them, and re-layouts: 78.2 us -> 3.18 us  [carried(): lax.dynamic_slice_in_dim(tensor, which * half, half, 0)]
    all_gather x4 -> x0, waiting for transfers between devices: 65.8 us -> none  [the longest x2 65.8 us: prefix(): lax.all_gather(part.astype(kind), axis)]
    ppermute x2 -> x13, waiting for transfers between devices: 1.87 us -> 53.6 us  [the longest x6 48.8 us: to_chip(): return lax.ppermute(value, 'seq', pairs)]
    reduce_sum x11 -> x2, other arithmetic: 51.5 us -> 1.69 us  [the longest x1 1.65 us: local(): jnp.sum(gw, axis=0)[:, :, :4]]
  transfers between devices with their start and end apart: 14 -> 21, of which waited for: 5 -> 14; matrix products, arithmetic and copies ran while one was open for 37% -> 17% of each run, Pallas kernels for 0% -> 7%
where the time goes in v1:
time: 847 us; the launch traced here: 836 us
  waiting for transfers between devices  329 us (39%)
  Pallas kernels  162 us (19%)
  matrix products  130 us (15%)
  local copies, waits for them, and re-layouts  73.5 us (9%)
  blocking collectives  68.7 us (8%)
  other arithmetic  32.4 us (4%)
  starting transfers between devices  24.2 us (3%)
  between operations  16.2 us (2%)
    reduce_scatter x5, waiting for transfers between devices, local(): lax.psum_scatter(shortened(mlp_terms + mixer_terms), 'seq', scatter_dimen...  204 us
    dot_general x17, matrix products, half_product(): return jnp.einsum(formula, former, latter, preferred_element_type=F32)  121 us
    pallas_call x1, Pallas kernels, maps(): pl.pallas_call(maps_kernel, grid=(rows, HEADS), in_specs=conv_specs(lengt...  68 us
    pallas_call x1, Pallas kernels, back(): pl.pallas_call(back_kernel, grid=(rows, HEADS), in_specs=conv_specs(lengt...  57.2 us
    psum x1, waiting for transfers between devices, local(): lax.psum(shortened(shards), 'row')  55.2 us
    ppermute x6, waiting for transfers between devices, to_chip(): return lax.ppermute(value, 'seq', pairs)  48.8 us
    psum x1, blocking collectives, local(): lax.psum((rate_sums[:, 0], rate_sums[:, 1], grad_out_gain), ('row', 'seq'))  38.7 us
    dynamic_update_slice x1, local copies, waits for them, and re-layouts, local(): lax.dynamic_update_slice_in_dim(grad_projected, tail, length - 8, 1)  28.5 us
  transfers between devices with their start and end apart: 21, of which 14 were waited for; matrix products, arithmetic and copies ran while one was open for 17% of the time, Pallas kernels for 7%

profile of v1, /device:TPU:0, one launch (start us, length us, event | category | flops | bytes accessed | tf_op | source)
XLA Modules:
  0.0 835.9 jit_solution(15847301190408299753)
XLA Ops:
  13.9 2.2 front.1
  16.1 10.3 %fusion.8.refs_0_.refs_1_.refs_2_.refs_3_.refs_4_ = bf16[2,256,5120]{2,1,0:T(8,128)(2,1)S(1)} fusion(bf16[2,256,1024]{2,1,0:T(8,128)(2,1)S(1)} %get-tuple-element.39, bf16[1024,5120]{1,0:T(8,128)(2,1)} %param.18), kind=kOutput, calls=%fused_computation.13 | convolution fusion | flops 5371330560 | bytes 16777216 | tf_op jit(solution)/shard_map/rld,de->rle/dot_general | solution.py:715
  26.5 2.3 copy-done.40
  28.8 2.4 collective-permute-start
  34.4 1.6 and_select_fusion.refs_18_
  41.1 68.0 %maps.1 = (bf16[2,8,256,128]{3,2,1,0:T(8,128)(2,1)S(1)}, bf16[2,8,2,256,128]{4,3,2,1,0:T(8,128)(2,1)}, bf16[2,8,2,256,128]{4,3,2,1,0:T(8,128)(2,1)}, bf16[2,8,2,...) custom-call(bf16[2,256,5120]{2,1,0:T(8,128)(2,1)} %copy-done.40, ...), custom_call_target="tpu_custom_call" | custom-call | tf_op jit(solution)/shard_map/maps/pallas_call | solution.py:270
  112.0 2.7 collective-permute-start.1
  117.2 1.5 fusion.96
  118.7 3.6 collective-permute-start.3
  123.6 4.7 collective-permute-done.3
  128.5 4.5 collective-permute-start.4
  133.0 5.0 collective-permute-done.4
  138.2 4.4 collective-permute-start.5
  142.7 4.1 collective-permute-done.5
  147.2 2.6 fusion.31.gate_ref
  151.0 17.9 %mix.1 = (bf16[2,256,1024]{2,1,0:T(8,128)(2,1)S(1)}, f32[2,256,1024]{2,1,0:T(8,128)S(1)}, bf16[2,8,2,128,128]{4,3,2,1,0:T(8,128)(2,1)S(1)}, bf16[2,8,2,256,128]{4,3,2,1,0:T(8,128)(2,1)}) custom-call(bf16[2,8,256,128]{3,2,1,0:T(8,128)(2,1)S(1)} %copy-done.3, bf16[2,8,2,256,128]{4,3,2,1,0:T(8,128)(2,1)} %get-tuple-element.43.k_ref.refs_21_, ...), custom_call_target="tpu_custom_call" | custom-call | tf_op jit(solution)/shard_map/mix/pallas_call | solution.py:339
  169.0 1.4 multiply_reduce_fusion.2
  170.7 13.9 %fusion.2 = f32[2,256,5632]{2,1,0:T(8,128)} fusion(bf16[1024,5632]{1,0:T(8,128)(2,1)} %param.27, f32[2,256,1024]{2,1,0:T(8,128)S(1)} %get-tuple-element.105, f32[1024]{0:T(1024)S(1)} %convert_element_type.249, f32[2,256]{1,0:T(2,128)S(1)} %fusion.88), kind=kOutput, calls=%fused_computation.5 | convolution fusion | flops 5907152896 | bytes 25171968 | tf_op jit(solution)/shard_map/rld,de->rle/dot_general | solution.py:715
  184.6 12.7 %fusion.54 = (f32[2,256,2816]{2,1,0:T(8,128)}, f32[2,256,2816]{2,1,0:T(8,128)}, bf16[2,256,2816]{2,1,0:T(8,128)(2,1)}) fusion(f32[2,256,5632]{2,1,0:T(8,128)} %fusion.2, bf16[2,256,1024]{2,1,0:T(8,128)(2,1)S(1)} %copy-done.50, bf16[2816,1024]{1,0:T(8,128)(2,1)} %param.28), kind=kOutput, calls=%fused_computation.86 | convolution fusion | flops 2972975104 | bytes 32768000 | tf_op jit(solution)/shard_map/rld,fd->rlf/dot_general | solution.py:715
  197.3 14.5 %multiply_reduce_fusion = (bf16[1024]{0:T(1024)(128)(2,1)}, f32[2,256]{1,0:T(2,128)S(1)}, f32[2,256,1024]{2,1,0:T(8,128)}) fusion(f32[2,256,1024]{2,1,0:T(8,128)} %copy-done.46, f32[2,256]{1,0:T(2,128)S(1)} %fusion.88, f32[1024]{0:T(1024)S(1)} %convert_element_type.249, bf16[1024,5632]{1,0:T(8,128)(2,1)} %param.27, f32[2,256,2816]{2,1,0:T(8,128)} %get-tuple-element.85, ...), kind=kOutput, calls=%fused_computation.47 | convolution fusion | flops 5914491392 | bytes 27273216 | tf_op jit(solution)/shard_map/rle,de->rld/dot_general | solution.py:715
  211.8 3.2 fusion.18
  215.1 2.7 fusion.25.up_ref
  217.8 16.7 %adjoint.1 = (bf16[2,256,1024]{2,1,0:T(8,128)(2,1)S(1)}, bf16[2,256,1024]{2,1,0:T(8,128)(2,1)S(1)}, f32[2,8,8,128]{3,2,1,0:T(8,128)S(1)}, bf16[2,8,128,128]{3,2,1,0:T(8,128)(2,1)S(1)}) custom-call(f32[2,256,1024]{2,1,0:T(8,128)} %fusion.25.up_ref, f32[2,256,1024]{2,1,0:T(8,128)} %copy-done.23, f32[2,256,1024]{2,1,0:T(8,128)} %fusion.31.gate_ref, ...), custom_call_target="tpu_custom_call" | custom-call | tf_op jit(solution)/shard_map/adjoint/pallas_call | solution.py:412
  237.2 2.7 bitcast_convert_fusion.4
  239.9 4.6 bitcast_convert_fusion.3
  244.6 7.7 bitcast_convert_fusion.2
  252.4 1.7 constant_dynamic-slice_fusion
  254.5 1.5 collective-permute-done.7
  256.0 1.7 fusion.97
  257.7 1.4 collective-permute-start.8
  260.4 13.9 %collective-permute-done.8 = bf16[1,8,128,128]{3,2,1,0:T(8,128)(2,1)S(1)} collective-permute-done((bf16[1,8,128,128]{3,2,1,0:T(8,128)(2,1)S(1)}, bf16[1,8,128,128]{3,2,1,0:T(8,128)(2,1)S(1)}, u32[]{:S(2)}, u32[]{:S(2)}) %collective-permute-start.8) | collective-permute-done | bytes 262176 | tf_op jit(solution)/shard_map/ppermute | solution.py:667
  274.6 1.3 collective-permute-start.9
  275.9 8.7 %collective-permute-done.9 = bf16[1,8,128,128]{3,2,1,0:T(8,128)(2,1)S(1)} collective-permute-done((bf16[1,8,128,128]{3,2,1,0:T(8,128)(2,1)S(1)}, bf16[1,8,128,128]{3,2,1,0:T(8,128)(2,1)S(1)}, u32[]{:S(2)}, u32[]{:S(2)}) %collective-permute-start.9) | collective-permute-done | bytes 262176 | tf_op jit(solution)/shard_map/ppermute | solution.py:667
  285.0 1.6 collective-permute-start.10
  286.6 12.3 %collective-permute-done.10 = bf16[1,8,128,128]{3,2,1,0:T(8,128)(2,1)S(1)} collective-permute-done((bf16[1,8,128,128]{3,2,1,0:T(8,128)(2,1)S(1)}, bf16[1,8,128,128]{3,2,1,0:T(8,128)(2,1)S(1)}, u32[]{:S(2)}, u32[]{:S(2)}) %collective-permute-start.10) | collective-permute-done | bytes 262176 | tf_op jit(solution)/shard_map/ppermute | solution.py:667
  298.9 1.3 broadcast_select_fusion
  300.3 1.5 collective-permute-done.11
  302.0 57.2 %back.1 = (bf16[5,2,256,1024]{3,2,1,0:T(8,128)(2,1)}, bf16[5,2,8,1024]{3,2,1,0:T(8,128)(2,1)}, f32[2,5,8,8,128]{4,3,2,1,0:T(8,128)S(1)}, f32[2,24,256]{2,1,0:T(8,128)S(1)}) custom-call(bf16[2,256,5120]{2,1,0:T(8,128)(2,1)} %copy-done.40, bf16[2,256,5120]{2,1,0:T(8,128)(2,1)} %copy-done.40, bf16[2,256,5120]{2,1,0:T(8,128)(2,1)} %copy-done.40, ...), custom_call_target="tpu_custom_call" | custom-call | tf_op jit(solution)/shard_map/back/pallas_call | solution.py:583
  359.9 1.3 collective-permute-start.12
  361.2 8.3 copy.103
  369.5 4.0 slice.70
  373.6 2.1 copy.126
  377.4 2.8 copy.106
  380.2 28.5 %dynamic_update_slice.3 = bf16[2,256,5120]{1,2,0:T(8,128)(2,1)} dynamic-update-slice(bf16[2,256,5120]{1,2,0:T(8,128)(2,1)} %bitcast.275, bf16[2,8,5120]{1,2,0:T(8,128)(2,1)} %copy.106, s32[]{:T(128)} %constant.90.clone.1, s32[]{:T(128)} %constant.108.clone.1, s32[]{:T(128)} %constant.90.clone.1) | dynamic-update-slice | bytes 327684 | tf_op jit(solution)/shard_map/dynamic_update_slice | solution.py:800
  408.6 10.3 %bitcast_convert_fusion.1 = bf16[1024,5120]{1,0:T(8,128)(2,1)} fusion(bf16[2,256,1024]{2,1,0:T(8,128)(2,1)} %copy-done.31, bf16[2,256,5120]{1,2,0:T(8,128)(2,1)} %dynamic_update_slice.3), kind=kOutput, calls=%fused_computation.1 | convolution fusion | flops 5373952000 | bytes 16777216 | tf_op jit(solution)/shard_map/rld,rle->de/dot_general | solution.py:715
  418.9 13.7 %bitcast_convert_fusion = bf16[1024,5632]{1,0:T(8,128)(2,1)} fusion(f32[2,256,2816]{2,1,0:T(8,128)} %get-tuple-element.85, f32[2,256,2816]{2,1,0:T(8,128)} %get-tuple-element.84, f32[2,256,1024]{2,1,0:T(8,128)} %copy-done.46, f32[1024]{0:T(1024)S(1)} %convert_element_type.249, f32[2,256]{1,0:T(2,128)S(1)} %fusion.88), kind=kOutput, calls=%fused_computation | convolution fusion | flops 5918687232 | bytes 25171968 | tf_op jit(solution)/shard_map/rld,rle->de/dot_general | solution.py:715
  433.6 1.7 reduce_sum.113
  435.2 1.5 slice.95
  436.7 2.3 copy.121
  440.2 1.5 fusion.53
  445.3 84.2 %reduce-scatter.12.cloned.1.call-done = bf16[128,5120]{1,0:T(8,128)(2,1)} async-done(((bf16[1024,5120]{1,0:T(8,128)(2,1)}), bf16[128,5120]{1,0:T(8,128)(2,1)}) %reduce-scatter.12.cloned.1.call-update) | async-done | bytes 1310736 | tf_op jit(solution)/shard_map/reduce_scatter | solution.py:818
  529.5 119.9 %reduce-scatter.18.cloned.1.call-done = bf16[128,5632]{1,0:T(8,128)(2,1)} async-done(((bf16[1024,5632]{1,0:T(8,128)(2,1)}), bf16[128,5632]{1,0:T(8,128)(2,1)}) %reduce-scatter.18.cloned.1.call-update) | async-done | bytes 1441808 | tf_op jit(solution)/shard_map/reduce_scatter | solution.py:818
  649.4 8.2 add_convert_fusion.1
  657.8 38.7 %all-reduce.6 = (f32[8]{0:T(128)}, f32[8]{0:T(128)}, f32[128]{0:T(128)}) all-reduce(f32[8]{0:T(128)S(1)} %get-tuple-element.69, f32[8]{0:T(128)S(1)} %get-tuple-element.68, f32[128]{0:T(128)S(1)} %reduce_sum.114), channel_id=1, replica_groups=mesh['row'=4,'seq'=8] {'row','seq'}, use_global_device_ids=true, to_apply=%region_17.18 | all-reduce | flops 144 | bytes 1152 | tf_op jit(solution)/shard_map/psum | solution.py:815
  696.5 1.8 fusion.75
  699.3 16.0 %reduce-scatter.24.cloned.1.call-done = bf16[128,24]{1,0:T(8,128)(2,1)} async-done(((bf16[1024,24]{1,0:T(8,128)(2,1)}), bf16[128,24]{1,0:T(8,128)(2,1)}) %reduce-scatter.24.cloned.1.call-update) | async-done | bytes 6160
  716.2 10.1 %fusion.4 = f32[2,256,1024]{2,1,0:T(8,128)S(1)} fusion(bf16[2,256,5120]{1,2,0:T(8,128)(2,1)} %dynamic_update_slice.3, bf16[1024,5120]{1,0:T(8,128)(2,1)} %param.18), kind=kOutput, calls=%fused_computation.8 | convolution fusion | flops 5368709120 | bytes 17825792 | tf_op jit(solution)/shard_map/rle,de->rld/dot_general | solution.py:715
  726.3 3.0 fusion.24
  729.3 13.7 %all-reduce.7 = (bf16[1024]{0:T(1024)(128)(2,1)S(1)}, bf16[1024]{0:T(1024)(128)(2,1)S(1)}) all-reduce(bf16[1024]{0:T(1024)(128)(2,1)S(1)} %get-tuple-element.66, bf16[1024]{0:T(1024)(128)(2,1)S(1)} %copy-done.58), channel_id=2, replica_groups=mesh['row'=4,'seq'=8] {'seq'}, use_global_device_ids=true, to_apply=%region_8.9.clone | all-reduce | flops 2048 | bytes 8192
  743.2 16.2 %all-reduce.8 = (bf16[128]{0:T(256)(128)(2,1)S(1)}, bf16[640,4]{0,1:T(4,128)(2,1)S(1)}, bf16[128,24]{0,1:T(8,128)(2,1)S(1)}, bf16[128]{0:T(256)(128)(2,1)S(1)}) all-reduce(bf16[128]{0:T(256)(128)(2,1)S(1)} %dynamic-slice.5, bf16[640,4]{0,1:T(4,128)(2,1)S(1)} %copy.122, ...), channel_id=1, replica_groups=mesh['row'=4,'seq'=8] {'row'}, use_global_device_ids=true, to_apply=%region_9.10 | all-reduce | flops 5888 | bytes 23552 | tf_op jit(solution)/shard_map/psum | solution.py:822
  761.7 3.8 fusion.20
  765.4 55.2 %all-reduce.12.cloned.1.call-done = (bf16[128,5120]{1,0:T(8,128)(2,1)}, bf16[128,1024]{1,0:T(8,128)(2,1)}, bf16[128,1024]{1,0:T(8,128)(2,1)}, bf16[128,5632]{1,0:T(8,128)(2,1)}, bf16[352,1024]{1,0:T(8,128)(2,1)}) async-done(((bf16[128,5120]{1,0:T(8,128)(2,1)}, bf16[128,1024]{1,0:T(8,128)(2,1)}, bf16[128,1024]{1,0:T(8,128)(2,1)}, bf16[128,5632]{1,0:T(8,128)(2,1)}, bf16[352,1024]{1,0:T(8,128)(2,1)}), ...) | async-done | bytes 3997712 | tf_op jit(solution)/shard_map/psum | solution.py:822
  820.6 3.2 convert_element_type.272
  825.5 1.9 convert_element_type.285
  (226 shorter events, 44.2 us)
Async XLA Ops:
  7.2 140.0 %copy-start = (bf16[1024,1024]{1,0:T(8,128)(2,1)S(1)}, bf16[1024,1024]{1,0:T(8,128)(2,1)}, u32[]{:S(2)}) copy-start(bf16[1024,1024]{1,0:T(8,128)(2,1)} %param.23) | copy-start | bytes 6291460
  7.2 6.7 copy-start.1
  7.2 438.1 %reduce-scatter.14.cloned.1.call-start = ((), (), s32[]{:S(2)}) async-start(), calls=%async_computation.8 | async-start | bytes 2359296 | tf_op jit(solution)/shard_map/reduce_scatter | solution.py:818
  8.2 18.2 %copy-start.35 = (f32[1024]{0:T(1024)}, f32[1024]{0:T(1024)S(1)}, u32[]{:S(2)}) copy-start(f32[1024]{0:T(1024)S(1)} %convert_element_type.229) | copy-start | bytes 12292
  16.1 10.4 %copy-start.8 = (f32[2,256,128]{2,1,0:T(8,128)}, f32[2,256,128]{2,1,0:T(8,128)S(1)}, u32[]{:S(2)}) copy-start(f32[2,256,128]{2,1,0:T(8,128)S(1)} %get-tuple-element.40.refs_16_.col_ref) | copy-start | bytes 786436
  16.1 10.4 %copy-start.13 = (f32[2,128,256]{2,1,0:T(8,128)}, f32[2,128,256]{2,1,0:T(8,128)S(1)}, u32[]{:S(2)}) copy-start(f32[2,128,256]{2,1,0:T(8,128)S(1)} %get-tuple-element.41.refs_17_.row_ref) | copy-start | bytes 786436
  16.1 10.4 %copy-start.31 = (bf16[2,256,1024]{2,1,0:T(8,128)(2,1)}, bf16[2,256,1024]{2,1,0:T(8,128)(2,1)S(1)}, u32[]{:S(2)}) copy-start(bf16[2,256,1024]{2,1,0:T(8,128)(2,1)S(1)} %get-tuple-element.39) | copy-start | bytes 3145732
  28.8 8.3 collective-permute-start
  37.0 72.0 %copy-start.19 = (s32[256,256]{1,0:T(8,128)}, s32[256,256]{1,0:T(8,128)S(1)}, u32[]{:S(2)}) copy-start(s32[256,256]{1,0:T(8,128)S(1)} %add_select_fusion.refs_19_) | copy-start | bytes 786436
  38.1 71.0 %copy-start.6 = (f32[2,3,256,128]{3,2,1,0:T(8,128)}, f32[2,3,256,128]{3,2,1,0:T(8,128)S(1)}, u32[]{:S(2)}) copy-start(f32[2,3,256,128]{3,2,1,0:T(8,128)S(1)} %broadcast_in_dim.86.refs_15_) | copy-start | bytes 2359300
  111.1 3.5 copy-start.41
  111.1 4.2 copy-start.47
  112.0 4.2 collective-permute-start.1
  115.3 1.9 collective-permute-start.2
  115.4 7.0 copy-start.42
  118.7 28.0 %copy-start.48 = (bf16[1,2,8,128,128]{4,3,2,1,0:T(8,128)(2,1)S(1)}, bf16[1,2,8,128,128]{4,3,2,1,0:T(8,128)(2,1)}, u32[]{:S(2)}) copy-start(bf16[1,2,8,128,128]{4,3,2,1,0:T(8,128)(2,1)} %copy-done.47) | copy-start | bytes 1572868
  118.7 9.5 %collective-permute-start.3 = (bf16[1,8,128,128]{3,2,1,0:T(8,128)(2,1)S(1)}, bf16[1,8,128,128]{3,2,1,0:T(8,128)(2,1)S(1)}, u32[]{:S(2)}, u32[]{:S(2)}) collective-permute-start(bf16[1,8,128,128]{3,2,1,0:T(8,128)(2,1)S(1)} %get-tuple-element.100), channel_id=1, source_target_pairs={{0,2},{1,3},{2,4},{3,5},{4,6},{5,7},{8,10},{9,11},{10,12},{11,13},... | collective-permute-start | bytes 786440 | tf_op jit(solution)/shard_map/ppermute | solution.py:667
  128.2 18.9 %copy-start.32 = (bf16[2,256,1024]{2,1,0:T(8,128)(2,1)S(1)}, bf16[2,256,1024]{2,1,0:T(8,128)(2,1)}, u32[]{:S(2)}) copy-start(bf16[2,256,1024]{2,1,0:T(8,128)(2,1)} %copy-done.31) | copy-start | bytes 3145732
  128.5 9.6 %collective-permute-start.4 = (bf16[1,8,128,128]{3,2,1,0:T(8,128)(2,1)S(1)}, bf16[1,8,128,128]{3,2,1,0:T(8,128)(2,1)S(1)}, u32[]{:S(2)}, u32[]{:S(2)}) collective-permute-start(bf16[1,8,128,128]{3,2,1,0:T(8,128)(2,1)S(1)} %fusion.52), channel_id=1, source_target_pairs={{0,2},{1,3},{2,4},{3,5},{4,6},{5,7},{8,10},{9,11},{10,12},{11,13},... | collective-permute-start | bytes 786440 | tf_op jit(solution)/shard_map/ppermute | solution.py:667
  138.2 8.5 %collective-permute-start.5 = (bf16[1,8,128,128]{3,2,1,0:T(8,128)(2,1)S(1)}, bf16[1,8,128,128]{3,2,1,0:T(8,128)(2,1)S(1)}, u32[]{:S(2)}, u32[]{:S(2)}) collective-permute-start(bf16[1,8,128,128]{3,2,1,0:T(8,128)(2,1)S(1)} %fusion.51), channel_id=1, source_target_pairs={{0,2},{1,3},{2,4},{3,5},{4,6},{5,7},{8,10},{9,11},{10,12},{11,13},... | collective-permute-start | bytes 786440 | tf_op jit(solution)/shard_map/ppermute | solution.py:667
  147.0 2.7 copy-start.57
  147.0 2.7 copy-start.62
  147.1 2.7 collective-permute-start.6
  151.0 17.9 %copy-start.60 = (bf16[1024,1024]{1,0:T(8,128)(2,1)S(1)}, bf16[1024,1024]{1,0:T(8,128)(2,1)}, u32[]{:S(2)}) copy-start(bf16[1024,1024]{1,0:T(8,128)(2,1)} %param.25) | copy-start | bytes 6291460
  168.9 15.6 %copy-start.39 = (bf16[2,256,1024]{2,1,0:T(8,128)(2,1)}, bf16[2,256,1024]{2,1,0:T(8,128)(2,1)S(1)}, u32[]{:S(2)}) copy-start(bf16[2,256,1024]{2,1,0:T(8,128)(2,1)S(1)} %get-tuple-element.47) | copy-start | bytes 3145732
  170.7 13.9 %copy-start.46 = (f32[2,256,1024]{2,1,0:T(8,128)}, f32[2,256,1024]{2,1,0:T(8,128)S(1)}, u32[]{:S(2)}) copy-start(f32[2,256,1024]{2,1,0:T(8,128)S(1)} %get-tuple-element.105) | copy-start | bytes 6291460
  170.7 13.9 %copy-start.50 = (bf16[2,256,1024]{2,1,0:T(8,128)(2,1)S(1)}, bf16[2,256,1024]{2,1,0:T(8,128)(2,1)}, u32[]{:S(2)}) copy-start(bf16[2,256,1024]{2,1,0:T(8,128)(2,1)} %param.29) | copy-start | bytes 3145732
  211.8 3.2 copy-start.61
  215.0 2.7 copy-start.45
  217.7 19.5 %copy-start.33 = (bf16[2,256,1024]{2,1,0:T(8,128)(2,1)S(1)}, bf16[2,256,1024]{2,1,0:T(8,128)(2,1)}, u32[]{:S(2)}) copy-start(bf16[2,256,1024]{2,1,0:T(8,128)(2,1)} %copy-done.31) | copy-start | bytes 3145732
  239.9 205.4 %reduce-scatter.16.cloned.1.call-start = ((), (), s32[]{:S(2)}) async-start(), calls=%async_computation.9 | async-start | bytes 2359296 | tf_op jit(solution)/shard_map/reduce_scatter | solution.py:818
  244.5 200.8 %reduce-scatter.20.cloned.1.call-start = ((), (), s32[]{:S(2)}) async-start(), calls=%async_computation.11 | async-start | bytes 6488064 | tf_op jit(solution)/shard_map/reduce_scatter | solution.py:818
  252.3 277.2 %reduce-scatter.12.cloned.1.call-start = ((), (), s32[]{:S(2)}) async-start(), calls=%async_computation.7 | async-start | bytes 11796480 | tf_op jit(solution)/shard_map/reduce_scatter | solution.py:818
  254.0 2.0 collective-permute-start.7
  254.5 4.6 copy-start.43
  257.7 41.2 %copy-start.22 = (bf16[2,8,128,128]{3,2,1,0:T(8,128)(2,1)S(1)}, bf16[2,8,128,128]{3,2,1,0:T(8,128)(2,1)}, u32[]{:S(2)}) copy-start(bf16[2,8,128,128]{3,2,1,0:T(8,128)(2,1)} %copy-done.21) | copy-start | bytes 1572868
  257.7 16.6 %collective-permute-start.8 = (bf16[1,8,128,128]{3,2,1,0:T(8,128)(2,1)S(1)}, bf16[1,8,128,128]{3,2,1,0:T(8,128)(2,1)S(1)}, u32[]{:S(2)}, u32[]{:S(2)}) collective-permute-start(bf16[1,8,128,128]{3,2,1,0:T(8,128)(2,1)S(1)} %get-tuple-element.107), channel_id=1, source_target_pairs={{2,0},{3,1},{4,2},{5,3},{6,4},{7,5},{10,8},{11,9},{12,10},{13,11},... | collective-permute-start | bytes 786440 | tf_op jit(solution)/shard_map/ppermute | solution.py:667
  274.6 10.0 %collective-permute-start.9 = (bf16[1,8,128,128]{3,2,1,0:T(8,128)(2,1)S(1)}, bf16[1,8,128,128]{3,2,1,0:T(8,128)(2,1)S(1)}, u32[]{:S(2)}, u32[]{:S(2)}) collective-permute-start(bf16[1,8,128,128]{3,2,1,0:T(8,128)(2,1)S(1)} %fusion.49), channel_id=1, source_target_pairs={{2,0},{3,1},{4,2},{5,3},{6,4},{7,5},{10,8},{11,9},{12,10},{13,11},... | collective-permute-start | bytes 786440 | tf_op jit(solution)/shard_map/ppermute | solution.py:667
  284.9 17.0 %copy-start.5 = (bf16[2,8,256,128]{3,2,1,0:T(8,128)(2,1)S(1)}, bf16[2,8,256,128]{3,2,1,0:T(8,128)(2,1)}, u32[]{:S(2)}) copy-start(bf16[2,8,256,128]{3,2,1,0:T(8,128)(2,1)} %copy-done.2) | copy-start | bytes 3145732
  284.9 17.0 %copy-start.7 = (f32[2,3,256,128]{3,2,1,0:T(8,128)S(1)}, f32[2,3,256,128]{3,2,1,0:T(8,128)}, u32[]{:S(2)}) copy-start(f32[2,3,256,128]{3,2,1,0:T(8,128)} %copy-done.6) | copy-start | bytes 2359300
  285.0 17.0 %copy-start.12 = (f32[2,256,128]{2,1,0:T(8,128)S(1)}, f32[2,256,128]{2,1,0:T(8,128)}, u32[]{:S(2)}) copy-start(f32[2,256,128]{2,1,0:T(8,128)} %copy-done.8) | copy-start | bytes 786436
  285.0 17.0 %copy-start.15 = (f32[2,128,256]{2,1,0:T(8,128)S(1)}, f32[2,128,256]{2,1,0:T(8,128)}, u32[]{:S(2)}) copy-start(f32[2,128,256]{2,1,0:T(8,128)} %copy-done.13) | copy-start | bytes 786436
  285.0 17.0 %copy-start.18 = (f32[2,2,128,128]{3,2,1,0:T(8,128)S(1)}, f32[2,2,128,128]{3,2,1,0:T(8,128)}, u32[]{:S(2)}) copy-start(f32[2,2,128,128]{3,2,1,0:T(8,128)} %and_select_fusion.refs_18_) | copy-start | bytes 786436
  285.0 17.0 %copy-start.20 = (s32[256,256]{1,0:T(8,128)S(1)}, s32[256,256]{1,0:T(8,128)}, u32[]{:S(2)}) copy-start(s32[256,256]{1,0:T(8,128)} %copy-done.19) | copy-start | bytes 786436
  285.0 17.0 %copy-start.27 = (bf16[2,8,2,128,128]{4,3,2,1,0:T(8,128)(2,1)S(1)}, bf16[2,8,2,128,128]{4,3,2,1,0:T(8,128)(2,1)}, u32[]{:S(2)}) copy-start(bf16[2,8,2,128,128]{4,3,2,1,0:T(8,128)(2,1)} %copy-done.26) | copy-start | bytes 3145732
  285.0 13.9 %collective-permute-start.10 = (bf16[1,8,128,128]{3,2,1,0:T(8,128)(2,1)S(1)}, bf16[1,8,128,128]{3,2,1,0:T(8,128)(2,1)S(1)}, u32[]{:S(2)}, u32[]{:S(2)}) collective-permute-start(bf16[1,8,128,128]{3,2,1,0:T(8,128)(2,1)S(1)} %fusion.48), channel_id=1, source_target_pairs={{2,0},{3,1},{4,2},{5,3},{6,4},{7,5},{10,8},{11,9},{12,10},{13,11},... | collective-permute-start | bytes 786440 | tf_op jit(solution)/shard_map/ppermute | solution.py:667
  300.3 1.6 collective-permute-start.11
  359.9 15.7 %collective-permute-start.12 = (bf16[5,2,8,1024]{3,2,1,0:T(8,128)(2,1)}, bf16[5,2,8,1024]{3,2,1,0:T(8,128)(2,1)}, u32[]{:S(2)}, u32[]{:S(2)}) collective-permute-start(bf16[5,2,8,1024]{3,2,1,0:T(8,128)(2,1)} %get-tuple-element.57), channel_id=1, source_target_pairs={{1,0},{2,1},{3,2},{4,3},{5,4},{6,5},{7,6},{9,8},{10,9},{11,10},{12... | collective-permute-start | bytes 491528 | tf_op jit(solution)/shard_map/ppermute | solution.py:673
  418.9 230.4 %reduce-scatter.18.cloned.1.call-start = ((), (), s32[]{:S(2)}) async-start(), calls=%async_computation.10 | async-start | bytes 12976128 | tf_op jit(solution)/shard_map/reduce_scatter | solution.py:818
  432.6 6.4 copy-start.59
  432.7 6.5 copy-start.16
  432.7 265.6 %reduce-scatter.22.cloned.1.call-start = ((), (), s32[]{:S(2)}) async-start(), calls=%async_computation.12 | async-start | bytes 1474560
  440.2 275.2 %reduce-scatter.24.cloned.1.call-start = ((), (), s32[]{:S(2)}) async-start(), calls=%async_computation.13 | async-start | bytes 294912
  442.6 378.0 %all-reduce.12.cloned.1.call-start = ((), (), s32[]{:S(2)}) async-start(), calls=%async_computation.14 | async-start | bytes 7995392 | tf_op jit(solution)/shard_map/psum | solution.py:822
  649.4 8.3 copy-start.38
  649.4 47.1 %copy-start.54 = (bf16[1024,24]{0,1:T(8,128)(2,1)S(1)}, bf16[1024,24]{0,1:T(8,128)(2,1)}, u32[]{:S(2)}) copy-start(bf16[1024,24]{0,1:T(8,128)(2,1)} %param.20) | copy-start | bytes 147460
  716.2 10.1 %copy-start.25 = (bf16[2,256,1024]{2,1,0:T(8,128)(2,1)S(1)}, bf16[2,256,1024]{2,1,0:T(8,128)(2,1)}, u32[]{:S(2)}) copy-start(bf16[2,256,1024]{2,1,0:T(8,128)(2,1)} %copy-done.24) | copy-start | bytes 3145732
  716.2 10.1 %copy-start.36 = (f32[1024]{0:T(1024)S(1)}, f32[1024]{0:T(1024)}, u32[]{:S(2)}) copy-start(f32[1024]{0:T(1024)} %copy-done.35) | copy-start | bytes 12292
  716.2 10.1 %copy-start.44 = (f32[2,256,1024]{2,1,0:T(8,128)S(1)}, f32[2,256,1024]{2,1,0:T(8,128)}, u32[]{:S(2)}) copy-start(f32[2,256,1024]{2,1,0:T(8,128)} %fusion.75) | copy-start | bytes 6291460
  726.3 3.0 copy-start.58
  726.3 35.4 %copy-start.56 = (f32[2,256]{1,0:T(2,128)S(1)}, f32[2,256]{1,0:T(2,128)}, u32[]{:S(2)}) copy-start(f32[2,256]{1,0:T(2,128)} %fusion.21) | copy-start | bytes 6148
  820.6 3.2 copy-start.53
  820.6 4.1 copy-start.52
  820.6 4.9 copy-start.49
  (20 other events, 27.9 us)
Sparse Core Ops, SparseCore 0:
  240.0 39.4 reduce-scatter.13
  281.8 37.8 reduce-scatter.15
  321.9 66.4 reduce-scatter.19
  419.0 110.4 reduce-scatter.11
  531.6 117.6 reduce-scatter.17
  652.1 31.9 reduce-scatter.21
  686.9 28.4 reduce-scatter.23
  720.2 100.3 all-reduce.11
